TPU v7x, 128 devices: a whole 4x4x4 slice. The times are simulated.
128 devices in a mesh: node: 16 (over x, z), local: 8 (over y, core).
Axes of the slice: x: 4, y: 4, z: 4, core: 2. Of those that a mesh axis runs over, the one named last changes fastest.
Arguments:
- tokens: bfloat16 [2048, 3584], P(('node', 'local')), may hold values from -6 to 6
- cotangent: bfloat16 [2048, 3584], P(('node', 'local')), may hold values from -0.59765625 to 0.59765625
- node_routes: int32 [2048, 4], P(('node', 'local')), may hold values from 0 to 15, all different within a row; in each aligned block of 16 rows (0 to 15, 16 to 31, ...) at most 5 rows name the same one
- home_local: int32 [128, 16], P(('node', 'local')), may hold values from 0 to 3
- second_local: int32 [2048, 4], P(('node', 'local')), may hold values from 0 to 3
- gate_weights: bfloat16 [2048, 8], P(('node', 'local')), may hold values from 0.049804688 to 0.5
- gate_w: bfloat16 [128, 3584, 512], P(('node', 'local')), may hold values from -0.09375 to 0.09375
- up_w: bfloat16 [128, 3584, 512], P(('node', 'local')), may hold values from -0.09375 to 0.09375
- down_w: bfloat16 [128, 512, 3584], P(('node', 'local')), may hold values from -0.1875 to 0.1875
Outputs:
- d_tokens: bfloat16 [2048, 3584], P(('node', 'local'))
- d_gates: bfloat16 [2048, 8], P(('node', 'local'))
- d_gate_w: bfloat16 [128, 3584, 512], P(('node', 'local'))
- d_up_w: bfloat16 [128, 3584, 512], P(('node', 'local'))
- d_down_w: bfloat16 [128, 512, 3584], P(('node', 'local'))
Inputs may be any that keep to these rules, and one draw needn't show every extreme that they name: `node_routes`: each row names 4 different nodes; within the 16 rows of one device no node is named by more than 5 rows, a bound that some block reaches, so one device sends at most 5 rows to one node or one expert, and some device exactly 5.
All inputs are finite; a program needn't handle non-finite values.
Results may differ from a plain program's by a relative error of at most 0.014.
Values may be sent and summed in bfloat16 or wider, within the bound.
No kernel may reach another device: no remote copies, remote signals or barrier semaphores. Data moves between devices by JAX's collectives and lax.ppermute only.
A program may use at most 128 MiB of HBM per device.

v0:
```python
import jax
import jax.numpy as jnp
from jax import lax
from jax.experimental import pallas as pl
from jax.experimental.pallas import tpu as pltpu
from jax.sharding import PartitionSpec as P

BF = jnp.bfloat16
F32 = jnp.float32
TAIL = 128


def along_x(value, step):
    pairs = [(x * 4 + z, (x + step) % 4 * 4 + z) for x in range(4) for z in range(4)]
    return lax.ppermute(value, "node", pairs)


def along_z(value, step):
    pairs = [(x * 4 + z, x * 4 + (z + step) % 4) for x in range(4) for z in range(4)]
    return lax.ppermute(value, "node", pairs)


def along_y(value, step):
    pairs = [(y * 2 + c, (y + step) % 4 * 2 + c) for y in range(4) for c in range(2)]
    return lax.ppermute(value, "local", pairs)


def across(value):
    return lax.ppermute(value, "local", [(i, i ^ 1) for i in range(8)])


def dot(left, right, dims):
    return lax.dot_general(left, right, ((dims[0], dims[1]), ((), ())), preferred_element_type=F32)


def silu_parts(pre_gate):
    sigmoid = jax.nn.sigmoid(pre_gate)
    return (pre_gate * sigmoid, sigmoid * (1.0 + pre_gate * (1.0 - sigmoid)))


def exchange_z(parts, sign):
    return [parts[0]] + [along_z(parts[k], sign * k) for k in (1, 2, 3)]


def nn(left, right):
    return dot(left, right, ((1,), (0,)))


def nt(left, right):
    return dot(left, right, ((1,), (1,)))


def tn(left, right):
    return dot(left, right, ((0,), (0,)))


def vmem(count):
    return [pl.BlockSpec(memory_space=pltpu.VMEM)] * count


def start_kernel(core, tok, cot, routes, homes, second, weights, keep, send):
    rows, width = tok.shape
    half = width // 2
    nodes = homes.shape[1]
    first = core[0] == 0
    lane = lax.broadcasted_iota(jnp.int32, (TAIL, rows), 0)
    row_id = lax.broadcasted_iota(jnp.int32, (nodes, nodes), 0)
    col_id = lax.broadcasted_iota(jnp.int32, (nodes, nodes), 1)
    home_col = jnp.sum(jnp.where(row_id == col_id, homes[...], 0), axis=1, keepdims=True)
    node_id = lax.broadcasted_iota(jnp.int32, (nodes, rows), 0)
    tail = jnp.zeros((TAIL, rows), F32)
    for j in range(routes.shape[0]):
        node = routes[j : j + 1, :]
        home = jnp.sum(jnp.where(node_id == node, home_col, 0), axis=0, keepdims=True)
        other = lax.rem(home + jnp.maximum(second[j : j + 1, :], 1), 4)
        for k, pick in ((2 * j, home), (2 * j + 1, other)):
            weight = weights[k : k + 1, :].astype(F32)
            tail = tail + jnp.where(lane == node * 4 + pick, weight, 0.0)
    tail = tail.T.astype(BF)
    for out, is_left in ((keep, first), (send, jnp.logical_not(first))):
        out[:, :half] = jnp.where(is_left, tok[:, :half], tok[:, half:])
        out[:, half : half + TAIL] = tail
        out[:, half + TAIL :] = jnp.where(is_left, cot[:, :half], cot[:, half:])


def weight_kernel(core, gate, up, down, _, gate_own, gate_oth, up_own, up_oth, down_own, down_oth, sems):
    half = down_own.shape[1]
    copies = []
    for src, outs in ((gate, (gate_own, gate_oth)), (up, (up_own, up_oth))):
        for out, which in zip(outs, (core[0], 1 - core[0])):
            rows = pl.ds(pl.multiple_of(which * half, half), half)
            copies.append((src.at[rows, :], out.at[pl.ds(0, half), :]))
    for out, which in ((down_own, core[0]), (down_oth, 1 - core[0])):
        cols = pl.ds(pl.multiple_of(which * half, half), half)
        copies.append((down.at[:, cols], out))
    copies = [
        pltpu.make_async_copy(src, dst, sems.at[i]) for i, (src, dst) in enumerate(copies)
    ]
    for copy in copies:
        copy.start()
    for out in (gate_own, gate_oth, up_own, up_oth):
        out[half:, :] = jnp.zeros((out.shape[0] - half, out.shape[1]), BF)
    for copy in copies:
        copy.wait()


def stack_kernel(top, bottom, _, out):
    side = top.shape[0]
    out[:side, :] = top[...]
    out[side:, :] = bottom[...]


def per_device(
    tokens, cotangent, node_routes, home_local, second_local, gate_weights, gate_w, up_w, down_w
):
    tok, width = tokens.shape
    half = width // 2
    top = gate_weights.shape[1]
    cap = 5
    experts = lax.axis_size("node") * 4
    node = lax.axis_index("node")
    local = lax.axis_index("local")
    x_pos, z_pos = node // 4, node % 4
    core = local % 2
    first = core == 0
    my_expert = 4 * node + local // 2
    core_arg = core.astype(jnp.int32).reshape(1)
    anywhere = pl.BlockSpec(memory_space=pl.ANY)

    raw_keep, raw_send = pl.pallas_call(
        start_kernel,
        out_shape=[jax.ShapeDtypeStruct((tok, width + TAIL), BF)] * 2,
        in_specs=[pl.BlockSpec(memory_space=pltpu.SMEM)] + [pl.BlockSpec()] * 6,
        out_specs=vmem(2),
    )(
        core_arg,
        tokens,
        cotangent,
        node_routes.T,
        home_local,
        second_local.T,
        gate_weights.T,
    )
    chip = jnp.concatenate([raw_keep, across(raw_send)], axis=0)
    rows = jnp.concatenate(
        [chip, along_x(chip, 1), along_x(chip, -1), along_x(chip, 2)], axis=0
    )

    weights = rows[:, half : half + experts]
    count = rows.shape[0]
    groups = count // tok
    slots = groups * cap
    nearby = 4 * x_pos + (z_pos + jnp.arange(4, dtype=jnp.int32)) % 4
    in_node = (jnp.arange(experts, dtype=jnp.int32)[:, None] // 4 == nearby[None, :]).astype(BF)
    member = nn((weights != 0).astype(BF), in_node) > 0
    row = jnp.arange(count, dtype=jnp.int32)
    before = (row[:, None] // tok == row[None, :] // tok) & (row[:, None] > row[None, :])
    rank = nn(before.astype(BF), member.astype(BF)).astype(jnp.int32)
    group = row // tok
    place = ((group // 2 * 2 + (group + core) % 2) * cap)[:, None] + rank
    place = jnp.where(member, place, -1)
    select = (
        (place.T[:, None, :] == jnp.arange(slots, dtype=jnp.int32)[None, :, None])
        .astype(BF)
        .reshape(4 * slots, count)
    )
    parts = jnp.split(nn(select, rows).astype(BF), 4, axis=0)
    side = 2 * slots

    hid_width = gate_w.shape[2]
    gate_own, gate_oth, up_own, up_oth, down_own, down_oth = pl.pallas_call(
        weight_kernel,
        out_shape=[jax.ShapeDtypeStruct((half + TAIL, hid_width), BF)] * 4
        + [jax.ShapeDtypeStruct((hid_width, half), BF)] * 2,
        in_specs=[pl.BlockSpec(memory_space=pltpu.SMEM)]
        + [pl.BlockSpec(memory_space=pltpu.HBM)] * 3
        + [anywhere],
        out_specs=vmem(6),
        scratch_shapes=[pltpu.SemaphoreType.DMA((6,))],
    )(core_arg, gate_w[0], up_w[0], down_w[0], raw_send)

    mine = jnp.concatenate(exchange_z(parts, 1), axis=0)
    below, above = along_y(mine, 1), along_y(mine, -1)
    far_parts = along_y(below[:side], 1), along_y(above[side:], -1)
    near = [mine, below, above]
    tail_lane = jnp.arange(TAIL, dtype=jnp.int32)[None, :]

    def row_gradients(own, oth):
        x_own, d_own = own[:, : half + TAIL], own[:, half + TAIL :]
        x_oth, d_oth = oth[:, : half + TAIL], oth[:, half + TAIL :]
        weight = jnp.sum(
            jnp.where(tail_lane == my_expert, x_own[:, half:].astype(F32), 0.0),
            axis=1,
            keepdims=True,
        )
        pre_gate = nn(x_own, gate_own) + nn(x_oth, gate_oth)
        pre_up = nn(x_own, up_own) + nn(x_oth, up_oth)
        activated, slope = silu_parts(pre_gate)
        hidden = (activated * pre_up).astype(BF)
        scaled = (weight * hidden.astype(F32)).astype(BF)
        hidden, scaled, for_gate, for_up = lax.optimization_barrier(
            (hidden, scaled, weight * (pre_up * slope), weight * activated)
        )
        hidden_grad = nt(d_own, down_own) + nt(d_oth, down_oth)
        gate_grad = (hidden_grad * for_gate).astype(BF)
        up_grad = (hidden_grad * for_up).astype(BF)
        got = across((nt(gate_grad, gate_oth) + nt(up_grad, up_oth)).astype(BF)[:, :half])
        keep = nt(gate_grad, gate_own) + nt(up_grad, up_own)
        router = jnp.sum(hidden_grad * hidden.astype(F32), axis=1)
        router = jnp.where(weight[:, 0] != 0, router, 0.0)
        router = (router + across(router))[:, None]
        high = router.astype(BF).astype(F32)
        tail = jnp.where(tail_lane == my_expert, high, 0.0)
        tail = jnp.where(tail_lane == my_expert + TAIL // 2, router - high, tail).astype(BF)
        full = (keep[:, :half] + got.astype(F32)).astype(BF)
        full = jnp.concatenate([full, tail], axis=1)
        pieces = lax.optimization_barrier(tuple(jnp.split(full, own.shape[0] // side, axis=0)))
        return (own, oth, gate_grad, up_grad, scaled), pieces

    near_state, pieces = row_gradients(
        jnp.concatenate(near, axis=0), jnp.concatenate([across(p) for p in near], axis=0)
    )
    own_top, own_bottom, below_top, below_bottom, above_top, above_bottom = pieces
    far = pl.pallas_call(
        stack_kernel,
        out_shape=jax.ShapeDtypeStruct((2 * side, rows.shape[1]), BF),
        in_specs=vmem(3),
        out_specs=vmem(1)[0],
    )(*far_parts, near_state[2])
    far_state, (far_top, far_bottom) = row_gradients(far, across(far))
    from_above = along_y(far_top, -1)
    from_below = along_y(far_bottom, 1)
    early_top, early_bottom = along_y(above_top, 1), along_y(below_bottom, -1)
    late_top = along_y(below_top + from_above, -1)
    late_bottom = along_y(above_bottom + from_below, 1)

    def add(*parts):
        return sum(p.astype(F32) for p in parts).astype(BF)

    top_rows = add(own_top, early_top, late_top)
    bottom_rows = add(own_bottom, early_bottom, late_bottom)
    back = [top_rows[:slots], top_rows[slots:], bottom_rows[:slots], bottom_rows[slots:]]
    back = jnp.concatenate(exchange_z(back, -1), axis=0)
    parts = jnp.split(tn(select, back).astype(BF), 4, axis=0)
    parts = [parts[0], along_x(parts[1], -1), along_x(parts[2], 1), along_x(parts[3], 2)]
    chip = sum(p.astype(F32) for p in parts)
    theirs = across(chip[tok:, :half].astype(BF))
    mine = chip[:tok]
    mine_cols = mine[:, :half].astype(BF)
    d_tokens = jnp.concatenate(
        [jnp.where(first, mine_cols, theirs), jnp.where(first, theirs, mine_cols)], axis=1
    )
    by_expert = mine[:, half : half + TAIL // 2] + mine[:, half + TAIL // 2 :]
    by_expert = jnp.concatenate([by_expert, jnp.zeros_like(by_expert)], axis=1)
    lane16 = jnp.arange(home_local.shape[1], dtype=jnp.int32)
    node_match = node_routes[:, :, None] == lane16[None, None, :]
    home = jnp.sum(jnp.where(node_match, home_local[0][None, None, :], 0), axis=2)
    other = (home + jnp.maximum(second_local, 1)) % 4
    ids = jnp.repeat(node_routes, 2, axis=1) * 4 + jnp.stack([home, other], axis=2).reshape(tok, top)
    onehot = ids[:, :, None] == jnp.arange(TAIL, dtype=jnp.int32)[None, None, :]
    d_gates = jnp.sum(jnp.where(onehot, by_expert[:, None, :], 0.0), axis=2).astype(BF)

    own, oth, gate_grad, up_grad, scaled = [
        jnp.concatenate(both, axis=0)
        for both in zip(near_state, far_state)
    ]

    def whole(mine, theirs):
        return jnp.where(
            first,
            jnp.concatenate([mine, theirs], axis=1),
            jnp.concatenate([theirs, mine], axis=1),
        )

    x_all = whole(own[:, :half], oth[:, :half])
    d_all = whole(own[:, half + TAIL :], oth[:, half + TAIL :])
    return (
        d_tokens,
        d_gates,
        tn(x_all, gate_grad).astype(BF)[None],
        tn(x_all, up_grad).astype(BF)[None],
        tn(scaled, d_all).astype(BF)[None],
    )


def solution(mesh):
    rows = P(("node", "local"), None)
    blocks = P(("node", "local"), None, None)
    return jax.shard_map(
        per_device,
        mesh=mesh,
        in_specs=(rows,) * 6 + (blocks,) * 3,
        out_specs=(rows, rows, blocks, blocks, blocks),
        check_vma=False,
    )
```

profile of v0, /device:TPU:1, one launch (start us, length us, event | category | flops | bytes accessed | tf_op | source)
XLA Modules:
  0.0 181.6 jit_solution(8798351470355755489)
XLA Ops:
  0.6 1.9 %shard_map.128 = (bf16[16,3712]{1,0:T(8,128)(2,1)}, bf16[16,3712]{1,0:T(8,128)(2,1)}) custom-call(s32[1]{0:T(128)} %bitcast.core, bf16[16,3584]{1,0:T(8,128)(2,1)} %tok.1, bf16[16,3584]{1,0:T(8,128)(2,1)} %cot.1, s32[4,16]{1,0:T(4,128)} %bitcast.60, s32[1,16]{1,0:T(1,128)} %homes.1, s32[4,16]{1,0:T(4,128)} %bitcast.62, bf16[8,16]{1,0:T(8,128)(2,1)} %bitcast.63), custom_call_target="tpu_custom_call" | custom-call | tf_op jit(solution)/shard_map/pallas_call | solution.py:130
  2.5 1.4 collective-permute-start
  4.6 0.9 constant_dynamic-update-slice_fusion.1
  5.6 0.9 select_reduce_fusion.3
  6.5 1.4 collective-permute-start.1
  8.7 2.5 %collective-permute-start.3 = (bf16[32,3712]{1,0:T(8,128)(2,1)S(1)}, bf16[32,3712]{1,0:T(8,128)(2,1)S(1)}, u32[]{:S(2)}, u32[]{:S(2)}) collective-permute-start(bf16[32,3712]{1,0:T(8,128)(2,1)S(1)} %get-tuple-element.117), channel_id=1, source_target_pairs={{0,64},{8,72},{16,80},{24,88},{32,96},{40,104},{48,112},{56,120},{... | collective-permute-start | bytes 712712 | tf_op jit(solution)/shard_map/ppermute | solution.py:15
  11.1 1.2 collective-permute-start.2
  12.3 2.9 %collective-permute-done.1 = bf16[32,3712]{1,0:T(8,128)(2,1)S(1)} collective-permute-done((bf16[32,3712]{1,0:T(8,128)(2,1)S(1)}, bf16[32,3712]{1,0:T(8,128)(2,1)S(1)}, u32[]{:S(2)}, u32[]{:S(2)}) %collective-permute-start.1) | collective-permute-done | bytes 237600 | tf_op jit(solution)/shard_map/ppermute | solution.py:15
  15.2 6.2 %collective-permute-done.2 = bf16[32,3712]{1,0:T(8,128)(2,1)S(1)} collective-permute-done((bf16[32,3712]{1,0:T(8,128)(2,1)S(1)}, bf16[32,3712]{1,0:T(8,128)(2,1)S(1)}, u32[]{:S(2)}, u32[]{:S(2)}) %collective-permute-start.2) | collective-permute-done | bytes 237600 | tf_op jit(solution)/shard_map/ppermute | solution.py:15
  22.5 0.9 constant_dynamic-update-slice_fusion.22
  23.4 3.8 %collective-permute-start.6 = (bf16[40,3712]{1,0:T(8,128)(2,1)S(1)}, bf16[40,3712]{1,0:T(8,128)(2,1)S(1)}, u32[]{:S(2)}, u32[]{:S(2)}) collective-permute-start(bf16[40,3712]{1,0:T(8,128)(2,1)S(1)} %get-tuple-element.81), channel_id=1, source_target_pairs={{0,24},{8,0},{16,8},{24,16},{32,56},{40,32},{48,40},{56,48},{64,88... | collective-permute-start | bytes 890888 | tf_op jit(solution)/shard_map/ppermute | solution.py:20
  28.1 8.6 %shard_map.129 = (bf16[1920,512]{1,0:T(8,128)(2,1)}, bf16[1920,512]{1,0:T(8,128)(2,1)}, bf16[1920,512]{1,0:T(8,128)(2,1)}, bf16[1920,512]{1,0:T(8,128)(2,1)}, bf...) custom-call(s32[1]{0:T(128)} %bitcast.core, bf16[3584,512]{1,0:T(8,128)(2,1)} %bitcast.56, bf16[3584,512]{1,0:T(8,128)(2,1)} %bitcast.57, ...), custom_call_target="tpu_custom_call" | custom-call | tf_op jit(solution)/shard_map/pallas_call | solution.py:171
  36.7 2.0 %collective-permute-done.6 = bf16[40,3712]{1,0:T(8,128)(2,1)S(1)} collective-permute-done((bf16[40,3712]{1,0:T(8,128)(2,1)S(1)}, bf16[40,3712]{1,0:T(8,128)(2,1)S(1)}, u32[]{:S(2)}, u32[]{:S(2)}) %collective-permute-start.6) | collective-permute-done | bytes 296992 | tf_op jit(solution)/shard_map/ppermute | solution.py:20
  38.8 4.7 %collective-permute-done.4 = bf16[40,3712]{1,0:T(8,128)(2,1)S(1)} collective-permute-done((bf16[40,3712]{1,0:T(8,128)(2,1)S(1)}, bf16[40,3712]{1,0:T(8,128)(2,1)S(1)}, u32[]{:S(2)}, u32[]{:S(2)}) %collective-permute-start.4) | collective-permute-done | bytes 296992 | tf_op jit(solution)/shard_map/ppermute | solution.py:20
  43.6 0.9 collective-permute-start.9
  44.5 2.7 %collective-permute-start.8 = (bf16[160,3712]{1,0:T(8,128)(2,1)S(1)}, bf16[160,3712]{1,0:T(8,128)(2,1)S(1)}, u32[]{:S(2)}, u32[]{:S(2)}) collective-permute-start(bf16[160,3712]{1,0:T(8,128)(2,1)S(1)} %pad_maximum_fusion), channel_id=1, source_target_pairs={{0,6},{1,7},{2,0},{3,1},{4,2},{5,3},{6,4},{7,5},{8,14},{9,15},{10,... | collective-permute-start | bytes 3563528 | tf_op jit(solution)/shard_map/ppermute | solution.py:25
  47.3 0.9 constant_dynamic-update-slice_fusion.21
  48.1 0.9 constant_dynamic-update-slice_fusion.20
  49.0 0.9 constant_dynamic-update-slice_fusion.19
  49.8 22.9 %collective-permute-done.8 = bf16[160,3712]{1,0:T(8,128)(2,1)S(1)} collective-permute-done((bf16[160,3712]{1,0:T(8,128)(2,1)S(1)}, bf16[160,3712]{1,0:T(8,128)(2,1)S(1)}, u32[]{:S(2)}, u32[]{:S(2)}) %collective-permute-start.8) | collective-permute-done | bytes 1187872 | tf_op jit(solution)/shard_map/ppermute | solution.py:25
  72.8 3.5 %collective-permute-start.16 = (bf16[80,3712]{1,0:T(8,128)(2,1)S(1)}, bf16[80,3712]{1,0:T(8,128)(2,1)S(1)}, u32[]{:S(2)}, u32[]{:S(2)}) collective-permute-start(bf16[80,3712]{1,0:T(8,128)(2,1)S(1)} %slice.135), channel_id=1, source_target_pairs={{0,6},{1,7},{2,0},{3,1},{4,2},{5,3},{6,4},{7,5},{8,14},{9,15},{10,... | collective-permute-start | bytes 1781768 | tf_op jit(solution)/shard_map/ppermute | solution.py:25
  76.4 1.2 collective-permute-start.11
  77.9 1.6 constant_dynamic-update-slice_fusion.18
  79.5 1.6 constant_dynamic-update-slice_fusion.17
  81.0 0.8 copy-done.2
  81.9 2.8 %fusion.22 = f32[480,512]{1,0:T(8,128)S(1)} fusion(bf16[1920,512]{1,0:T(8,128)(2,1)S(1)} %copy-done.2, bf16[480,3712]{1,0:T(8,128)(2,1)} %get-tuple-element.76), kind=kOutput, calls=%fused_computation.36 | convolution fusion | flops 943718400 | bytes 4792320 | tf_op jit(solution)/shard_map/dot_general | solution.py:33
  85.0 1.2 fusion.20
  86.5 1.1 fusion.14
  88.6 2.2 %copy-done.14 = bf16[640,3712]{1,0:T(8,128)(2,1)} copy-done((bf16[640,3712]{1,0:T(8,128)(2,1)}, bf16[640,3712]{1,0:T(8,128)(2,1)S(1)}, u32[]{:S(2)}) %copy-start.14) | copy-done | bytes 4751384
  90.8 1.2 fusion.24
  92.3 2.4 %multiply_convert_fusion.2 = (bf16[480,512]{1,0:T(8,128)(2,1)}, bf16[480,512]{1,0:T(8,128)(2,1)S(1)}, f32[480,512]{1,0:T(8,128)S(1)}, f32[480,512]{1,0:T(8,128)S(1)}) fusion(f32[480]{0:T(512)S(1)} %select_reduce_fusion, f32[480,512]{1,0:T(8,128)S(1)} %fusion.24, f32[480,512]{1,0:T(8,128)S(1)} %fusion.20, bf16[1920,512]{1,0:T(8,128)(2,1)S(1)} %copy-done.5, ...), kind=kOutput, calls=%fused_computation.63 | convolution fusion | flops 947896320 | bytes 8726528 | tf_op jit(solution)/shard_map/dot_general | solution.py:33
  94.7 1.3 multiply_reduce_fusion
  96.0 3.2 %fusion.102 = f32[480,1920]{1,0:T(8,128)} fusion(bf16[480,512]{1,0:T(8,128)(2,1)S(1)} %get-tuple-element.94._, bf16[1920,512]{1,0:T(8,128)(2,1)S(1)} %copy-done.2), kind=kOutput, calls=%fused_computation.215 | convolution fusion | flops 943718400 | bytes 6144000 | tf_op jit(solution)/shard_map/dot_general | solution.py:33
  99.2 3.0 %fusion.104 = f32[480,1920]{1,0:T(8,128)} fusion(bf16[480,512]{1,0:T(8,128)(2,1)S(1)} %get-tuple-element.94._, bf16[1920,512]{1,0:T(8,128)(2,1)S(1)} %copy-done.3), kind=kOutput, calls=%fused_computation.217 | convolution fusion | flops 943718400 | bytes 6144000 | tf_op jit(solution)/shard_map/dot_general | solution.py:33
  102.2 0.8 copy-done.17
  103.0 2.5 %shard_map.130 = bf16[160,3712]{1,0:T(8,128)(2,1)} custom-call(bf16[80,3712]{1,0:T(8,128)(2,1)} %collective-permute-done.15.top, bf16[80,3712]{1,0:T(8,128)(2,1)} %copy-done.17, bf16[480,512]{1,0:T(8,128)(2,1)} %copy-done.7), custom_call_target="tpu_custom_call" | custom-call | tf_op jit(solution)/shard_map/pallas_call | solution.py:224
  105.7 2.4 %constant_dynamic-update-slice_fusion.16 = bf16[640,3712]{1,0:T(8,128)(2,1)} fusion(bf16[640,3712]{1,0:T(8,128)(2,1)} %get-tuple-element.75, bf16[160,3712]{1,0:T(8,128)(2,1)} %shard_map.130), kind=kLoop, calls=%fused_computation.143 | loop fusion | bytes 2375680 | tf_op jit(solution)/shard_map/concatenate | solution.py:264
  108.1 2.8 %fusion.97 = (bf16[640,1792]{1,0:T(8,128)(2,1)S(1)}, bf16[640,1792]{1,0:T(8,128)(2,1)S(1)}) fusion(bf16[640,3712]{1,0:T(8,128)(2,1)} %constant_dynamic-update-slice_fusion.16), kind=kLoop, calls=%fused_computation.210 | loop fusion | bytes 9175040 | tf_op jit(solution)/shard_map/slice | solution.py:276
  111.2 1.2 fusion.105
  112.5 0.8 copy-done.1
  113.3 1.5 fusion.9
  115.5 1.2 fusion.103
  119.8 0.9 copy-done.13
  120.7 0.7 fusion.55
  121.5 0.9 multiply_reduce_fusion.1
  122.3 0.8 fusion.109
  123.1 0.8 fusion.107
  124.8 0.8 fusion.108
  125.7 0.8 fusion.106
  127.0 1.6 collective-permute-done.18
  128.8 2.8 %collective-permute-start.20 = (bf16[80,1920]{1,0:T(8,128)(2,1)S(1)}, bf16[80,1920]{1,0:T(8,128)(2,1)S(1)}, u32[]{:S(2)}, u32[]{:S(2)}) collective-permute-start(bf16[80,1920]{1,0:T(8,128)(2,1)S(1)} %get-tuple-element.46), channel_id=1, source_target_pairs={{0,6},{1,7},{2,0},{3,1},{4,2},{5,3},{6,4},{7,5},{8,14},{9,15},{10,... | collective-permute-start | bytes 921608 | tf_op jit(solution)/shard_map/ppermute | solution.py:25
  132.6 5.3 %collective-permute-done.20 = bf16[80,1920]{1,0:T(8,128)(2,1)S(1)} collective-permute-done((bf16[80,1920]{1,0:T(8,128)(2,1)S(1)}, bf16[80,1920]{1,0:T(8,128)(2,1)S(1)}, u32[]{:S(2)}, u32[]{:S(2)}) %collective-permute-start.20) | collective-permute-done | bytes 307232 | tf_op jit(solution)/shard_map/ppermute | solution.py:25
  137.9 3.5 %collective-permute-start.21 = (bf16[80,1920]{1,0:T(8,128)(2,1)S(1)}, bf16[80,1920]{1,0:T(8,128)(2,1)S(1)}, u32[]{:S(2)}, u32[]{:S(2)}) collective-permute-start(bf16[80,1920]{1,0:T(8,128)(2,1)S(1)} %add.248), channel_id=1, source_target_pairs={{0,6},{1,7},{2,0},{3,1},{4,2},{5,3},{6,4},{7,5},{8,14},{9,15},{10,... | collective-permute-start | bytes 921608 | tf_op jit(solution)/shard_map/ppermute | solution.py:25
  141.4 6.6 %fusion.1 = bf16[1,3584,512]{2,1,0:T(8,128)(2,1)} fusion(bf16[640,1792]{1,0:T(8,128)(2,1)S(1)} %get-tuple-element.67, bf16[640,1792]{1,0:T(8,128)(2,1)S(1)} %get-tuple-element.65, pred[]{:T(512)S(6)} %eq.114, bf16[160,512]{1,0:T(8,128)(2,1)S(1)} %get-tuple-element.103, bf16[480,512]{1,0:T(8,128)(2,1)S(1)} %get-tuple-element.93), kind=kOutput, calls=%fused_computation.4 | convolution fusion | flops 2372599808 | bytes 8912897 | tf_op jit(solution)/shard_map/dot_general | solution.py:33
  148.5 1.1 collective-permute-start.25
  149.8 0.7 collective-permute-start.22
  150.5 4.8 %collective-permute-done.23 = bf16[80,1920]{1,0:T(8,128)(2,1)S(1)} collective-permute-done((bf16[80,1920]{1,0:T(8,128)(2,1)S(1)}, bf16[80,1920]{1,0:T(8,128)(2,1)S(1)}, u32[]{:S(2)}, u32[]{:S(2)}) %collective-permute-start.23) | collective-permute-done | bytes 307232 | tf_op jit(solution)/shard_map/ppermute | solution.py:25
  155.3 1.7 collective-permute-done.25
  157.5 0.9 collective-permute-start.27
  158.4 6.6 %fusion = bf16[1,3584,512]{2,1,0:T(8,128)(2,1)} fusion(bf16[640,1792]{1,0:T(8,128)(2,1)S(1)} %get-tuple-element.67, bf16[640,1792]{1,0:T(8,128)(2,1)S(1)} %get-tuple-element.65, pred[]{:T(512)S(6)} %eq.114, bf16[160,512]{1,0:T(8,128)(2,1)S(1)} %get-tuple-element.104, bf16[480,512]{1,0:T(8,128)(2,1)S(1)} %copy-done.8), kind=kOutput, calls=%fused_computation.3 | convolution fusion | flops 2372599808 | bytes 8912897 | tf_op jit(solution)/shard_map/dot_general | solution.py:33
  165.1 1.5 collective-permute-done.27
  166.9 3.0 %collective-permute-start.28 = (bf16[32,1920]{1,0:T(8,128)(2,1)S(1)}, bf16[32,1920]{1,0:T(8,128)(2,1)S(1)}, u32[]{:S(2)}, u32[]{:S(2)}) collective-permute-start(bf16[32,1920]{1,0:T(8,128)(2,1)S(1)} %get-tuple-element.98), channel_id=1, source_target_pairs={{0,96},{8,104},{16,112},{24,120},{32,0},{40,8},{48,16},{56,24},{64... | collective-permute-start | bytes 368648 | tf_op jit(solution)/shard_map/ppermute | solution.py:15
  170.6 5.9 %fusion.2 = bf16[1,512,3584]{2,1,0:T(8,128)(2,1)} fusion(bf16[640,1792]{1,0:T(8,128)(2,1)S(1)} %get-tuple-element.66, bf16[640,1792]{1,0:T(8,128)(2,1)S(1)} %get-tuple-element.64, pred[]{:T(512)S(6)} %eq.114, bf16[160,512]{1,0:T(8,128)(2,1)S(1)} %get-tuple-element.52, bf16[480,512]{1,0:T(8,128)(2,1)S(1)} %copy-done.19), kind=kOutput, calls=%fused_computation.5 | convolution fusion | flops 2372599808 | bytes 8912897 | tf_op jit(solution)/shard_map/dot_general | solution.py:33
  176.7 3.4 %collective-permute-start.31 = (bf16[16,1792]{1,0:T(8,128)(2,1)S(1)}, bf16[16,1792]{1,0:T(8,128)(2,1)S(1)}, u32[]{:S(2)}, u32[]{:S(2)}) collective-permute-start(bf16[16,1792]{1,0:T(8,128)(2,1)S(1)} %slice.150), channel_id=1, source_target_pairs={{0,1},{1,0},{2,3},{3,2},{4,5},{5,4},{6,7},{7,6},{8,9},{9,8},{10,11... | collective-permute-start | bytes 172040 | tf_op jit(solution)/shard_map/ppermute | solution.py:29
  (141 shorter events, 16.7 us)
Async XLA Ops:
  2.5 4.0 %collective-permute-start = (bf16[16,3712]{1,0:T(8,128)(2,1)}, bf16[16,3712]{1,0:T(8,128)(2,1)S(1)}, u32[]{:S(2)}, u32[]{:S(2)}) collective-permute-start(bf16[16,3712]{1,0:T(8,128)(2,1)} %get-tuple-element.30._), channel_id=1, source_target_pairs={{0,1},{1,0},{2,3},{3,2},{4,5},{5,4},{6,7},{7,6},{8,9},{9,8},{10,11... | collective-permute-start | bytes 356360 | tf_op jit(solution)/shard_map/ppermute | solution.py:29
  6.5 8.7 %collective-permute-start.1 = (bf16[32,3712]{1,0:T(8,128)(2,1)S(1)}, bf16[32,3712]{1,0:T(8,128)(2,1)S(1)}, u32[]{:S(2)}, u32[]{:S(2)}) collective-permute-start(bf16[32,3712]{1,0:T(8,128)(2,1)S(1)} %get-tuple-element.117), channel_id=1, source_target_pairs={{0,32},{8,40},{16,48},{24,56},{32,64},{40,72},{48,80},{56,88},{64,... | collective-permute-start | bytes 712712 | tf_op jit(solution)/shard_map/ppermute | solution.py:15
  8.7 12.7 %collective-permute-start.3 = (bf16[32,3712]{1,0:T(8,128)(2,1)S(1)}, bf16[32,3712]{1,0:T(8,128)(2,1)S(1)}, u32[]{:S(2)}, u32[]{:S(2)}) collective-permute-start(bf16[32,3712]{1,0:T(8,128)(2,1)S(1)} %get-tuple-element.117), channel_id=1, source_target_pairs={{0,64},{8,72},{16,80},{24,88},{32,96},{40,104},{48,112},{56,120},{... | collective-permute-start | bytes 712712 | tf_op jit(solution)/shard_map/ppermute | solution.py:15
  11.1 10.3 %collective-permute-start.2 = (bf16[32,3712]{1,0:T(8,128)(2,1)S(1)}, bf16[32,3712]{1,0:T(8,128)(2,1)S(1)}, u32[]{:S(2)}, u32[]{:S(2)}) collective-permute-start(bf16[32,3712]{1,0:T(8,128)(2,1)S(1)} %get-tuple-element.117), channel_id=1, source_target_pairs={{0,96},{8,104},{16,112},{24,120},{32,0},{40,8},{48,16},{56,24},{64... | collective-permute-start | bytes 712712 | tf_op jit(solution)/shard_map/ppermute | solution.py:15
  23.4 15.3 %collective-permute-start.6 = (bf16[40,3712]{1,0:T(8,128)(2,1)S(1)}, bf16[40,3712]{1,0:T(8,128)(2,1)S(1)}, u32[]{:S(2)}, u32[]{:S(2)}) collective-permute-start(bf16[40,3712]{1,0:T(8,128)(2,1)S(1)} %get-tuple-element.81), channel_id=1, source_target_pairs={{0,24},{8,0},{16,8},{24,16},{32,56},{40,32},{48,40},{56,48},{64,88... | collective-permute-start | bytes 890888 | tf_op jit(solution)/shard_map/ppermute | solution.py:20
  27.3 11.5 %collective-permute-start.5 = (bf16[40,3712]{1,0:T(8,128)(2,1)S(1)}, bf16[40,3712]{1,0:T(8,128)(2,1)S(1)}, u32[]{:S(2)}, u32[]{:S(2)}) collective-permute-start(bf16[40,3712]{1,0:T(8,128)(2,1)S(1)} %get-tuple-element.82), channel_id=1, source_target_pairs={{0,16},{8,24},{16,0},{24,8},{32,48},{40,56},{48,32},{56,40},{64,80... | collective-permute-start | bytes 890888 | tf_op jit(solution)/shard_map/ppermute | solution.py:20
  27.3 16.2 %collective-permute-start.4 = (bf16[40,3712]{1,0:T(8,128)(2,1)S(1)}, bf16[40,3712]{1,0:T(8,128)(2,1)S(1)}, u32[]{:S(2)}, u32[]{:S(2)}) collective-permute-start(bf16[40,3712]{1,0:T(8,128)(2,1)S(1)} %get-tuple-element.83), channel_id=1, source_target_pairs={{0,8},{8,16},{16,24},{24,0},{32,40},{40,48},{48,56},{56,32},{64,72... | collective-permute-start | bytes 890888 | tf_op jit(solution)/shard_map/ppermute | solution.py:20
  43.6 44.2 %collective-permute-start.9 = (bf16[160,3712]{1,0:T(8,128)(2,1)S(1)}, bf16[160,3712]{1,0:T(8,128)(2,1)S(1)}, u32[]{:S(2)}, u32[]{:S(2)}) collective-permute-start(bf16[160,3712]{1,0:T(8,128)(2,1)S(1)} %pad_maximum_fusion), channel_id=1, source_target_pairs={{0,1},{1,0},{2,3},{3,2},{4,5},{5,4},{6,7},{7,6},{8,9},{9,8},{10,11... | collective-permute-start | bytes 3563528 | tf_op jit(solution)/shard_map/ppermute | solution.py:29
  44.5 28.2 %collective-permute-start.8 = (bf16[160,3712]{1,0:T(8,128)(2,1)S(1)}, bf16[160,3712]{1,0:T(8,128)(2,1)S(1)}, u32[]{:S(2)}, u32[]{:S(2)}) collective-permute-start(bf16[160,3712]{1,0:T(8,128)(2,1)S(1)} %pad_maximum_fusion), channel_id=1, source_target_pairs={{0,6},{1,7},{2,0},{3,1},{4,2},{5,3},{6,4},{7,5},{8,14},{9,15},{10,... | collective-permute-start | bytes 3563528 | tf_op jit(solution)/shard_map/ppermute | solution.py:25
  47.2 29.0 %collective-permute-start.7 = (bf16[160,3712]{1,0:T(8,128)(2,1)S(1)}, bf16[160,3712]{1,0:T(8,128)(2,1)S(1)}, u32[]{:S(2)}, u32[]{:S(2)}) collective-permute-start(bf16[160,3712]{1,0:T(8,128)(2,1)S(1)} %pad_maximum_fusion), channel_id=1, source_target_pairs={{0,2},{1,3},{2,4},{3,5},{4,6},{5,7},{6,0},{7,1},{8,10},{9,11},{10,... | collective-permute-start | bytes 3563528 | tf_op jit(solution)/shard_map/ppermute | solution.py:25
  72.8 29.4 %collective-permute-start.16 = (bf16[80,3712]{1,0:T(8,128)(2,1)S(1)}, bf16[80,3712]{1,0:T(8,128)(2,1)S(1)}, u32[]{:S(2)}, u32[]{:S(2)}) collective-permute-start(bf16[80,3712]{1,0:T(8,128)(2,1)S(1)} %slice.135), channel_id=1, source_target_pairs={{0,6},{1,7},{2,0},{3,1},{4,2},{5,3},{6,4},{7,5},{8,14},{9,15},{10,... | collective-permute-start | bytes 1781768 | tf_op jit(solution)/shard_map/ppermute | solution.py:25
  76.3 25.9 %collective-permute-start.15 = (bf16[80,3712]{1,0:T(8,128)(2,1)S(1)}, bf16[80,3712]{1,0:T(8,128)(2,1)}, u32[]{:S(2)}, u32[]{:S(2)}) collective-permute-start(bf16[80,3712]{1,0:T(8,128)(2,1)S(1)} %slice.134), channel_id=1, source_target_pairs={{0,2},{1,3},{2,4},{3,5},{4,6},{5,7},{6,0},{7,1},{8,10},{9,11},{10,... | collective-permute-start | bytes 1781768 | tf_op jit(solution)/shard_map/ppermute | solution.py:25
  76.4 11.9 %collective-permute-start.11 = (bf16[160,3712]{1,0:T(8,128)(2,1)S(1)}, bf16[160,3712]{1,0:T(8,128)(2,1)S(1)}, u32[]{:S(2)}, u32[]{:S(2)}) collective-permute-start(bf16[160,3712]{1,0:T(8,128)(2,1)S(1)} %collective-permute-done.8), channel_id=1, source_target_pairs={{0,1},{1,0},{2,3},{3,2},{4,5},{5,4},{6,7},{7,6},{8,9},{9,8},{10,11... | collective-permute-start | bytes 3563528 | tf_op jit(solution)/shard_map/ppermute | solution.py:29
  77.6 10.3 %collective-permute-start.10 = (bf16[160,3712]{1,0:T(8,128)(2,1)S(1)}, bf16[160,3712]{1,0:T(8,128)(2,1)S(1)}, u32[]{:S(2)}, u32[]{:S(2)}) collective-permute-start(bf16[160,3712]{1,0:T(8,128)(2,1)S(1)} %collective-permute-done.7), channel_id=1, source_target_pairs={{0,1},{1,0},{2,3},{3,2},{4,5},{5,4},{6,7},{7,6},{8,9},{9,8},{10,11... | collective-permute-start | bytes 3563528 | tf_op jit(solution)/shard_map/ppermute | solution.py:29
  79.5 2.4 %copy-start.2 = (bf16[1920,512]{1,0:T(8,128)(2,1)S(1)}, bf16[1920,512]{1,0:T(8,128)(2,1)}, u32[]{:S(2)}) copy-start(bf16[1920,512]{1,0:T(8,128)(2,1)} %get-tuple-element.33) | copy-start | bytes 5898244
  81.9 2.9 %copy-start.10 = (bf16[1920,512]{1,0:T(8,128)(2,1)S(1)}, bf16[1920,512]{1,0:T(8,128)(2,1)}, u32[]{:S(2)}) copy-start(bf16[1920,512]{1,0:T(8,128)(2,1)} %get-tuple-element.35) | copy-start | bytes 5898244
  81.9 3.2 %copy-start.18 = (bf16[480,3712]{1,0:T(8,128)(2,1)S(1)}, bf16[480,3712]{1,0:T(8,128)(2,1)}, u32[]{:S(2)}) copy-start(bf16[480,3712]{1,0:T(8,128)(2,1)} %get-tuple-element.76) | copy-start | bytes 10690564
  85.0 1.5 copy-start.15
  88.3 2.5 %copy-start.3 = (bf16[1920,512]{1,0:T(8,128)(2,1)S(1)}, bf16[1920,512]{1,0:T(8,128)(2,1)}, u32[]{:S(2)}) copy-start(bf16[1920,512]{1,0:T(8,128)(2,1)} %get-tuple-element.34) | copy-start | bytes 5898244
  88.6 2.2 %copy-start.14 = (bf16[640,3712]{1,0:T(8,128)(2,1)}, bf16[640,3712]{1,0:T(8,128)(2,1)S(1)}, u32[]{:S(2)}) copy-start(bf16[640,3712]{1,0:T(8,128)(2,1)S(1)} %get-tuple-element.85) | copy-start | bytes 14254084
  90.8 1.5 copy-start.5
  92.3 2.4 %copy-start.12 = (bf16[512,1792]{1,0:T(8,128)(2,1)S(1)}, bf16[512,1792]{1,0:T(8,128)(2,1)}, u32[]{:S(2)}) copy-start(bf16[512,1792]{1,0:T(8,128)(2,1)} %get-tuple-element.32) | copy-start | bytes 5505028
  96.0 3.2 %copy-start.7 = (bf16[480,512]{1,0:T(8,128)(2,1)}, bf16[480,512]{1,0:T(8,128)(2,1)S(1)}, u32[]{:S(2)}) copy-start(bf16[480,512]{1,0:T(8,128)(2,1)S(1)} %get-tuple-element.94._) | copy-start | bytes 1474564
  102.2 0.8 copy-start.17
  105.5 12.1 %collective-permute-start.17 = (bf16[160,3712]{1,0:T(8,128)(2,1)}, bf16[160,3712]{1,0:T(8,128)(2,1)S(1)}, u32[]{:S(2)}, u32[]{:S(2)}) collective-permute-start(bf16[160,3712]{1,0:T(8,128)(2,1)} %shard_map.130), channel_id=1, source_target_pairs={{0,1},{1,0},{2,3},{3,2},{4,5},{5,4},{6,7},{7,6},{8,9},{9,8},{10,11... | collective-permute-start | bytes 3563528 | tf_op jit(solution)/shard_map/ppermute | solution.py:29
  108.1 3.1 %copy-start.6 = (bf16[1920,512]{1,0:T(8,128)(2,1)S(1)}, bf16[1920,512]{1,0:T(8,128)(2,1)}, u32[]{:S(2)}) copy-start(bf16[1920,512]{1,0:T(8,128)(2,1)} %get-tuple-element.36) | copy-start | bytes 5898244
  110.9 6.5 %collective-permute-start.13 = (f32[480]{0:T(512)S(1)}, f32[480]{0:T(512)S(1)}, u32[]{:S(2)}, u32[]{:S(2)}) collective-permute-start(f32[480]{0:T(512)S(1)} %compare_select_fusion.5), channel_id=1, source_target_pairs={{0,1},{1,0},{2,3},{3,2},{4,5},{5,4},{6,7},{7,6},{8,9},{9,8},{10,11... | collective-permute-start | bytes 5768 | tf_op jit(solution)/shard_map/ppermute | solution.py:29
  111.2 2.0 %copy-start.1 = (f32[480,1920]{1,0:T(8,128)S(1)}, f32[480,1920]{1,0:T(8,128)}, u32[]{:S(2)}) copy-start(f32[480,1920]{1,0:T(8,128)} %fusion.104) | copy-start | bytes 11059204
  113.3 2.2 %copy-start.11 = (bf16[1920,512]{1,0:T(8,128)(2,1)S(1)}, bf16[1920,512]{1,0:T(8,128)(2,1)}, u32[]{:S(2)}) copy-start(bf16[1920,512]{1,0:T(8,128)(2,1)} %get-tuple-element.35) | copy-start | bytes 5898244
  115.5 1.3 copy-start.9
  115.5 2.1 %copy-start.4 = (bf16[1920,512]{1,0:T(8,128)(2,1)S(1)}, bf16[1920,512]{1,0:T(8,128)(2,1)}, u32[]{:S(2)}) copy-start(bf16[1920,512]{1,0:T(8,128)(2,1)} %get-tuple-element.34) | copy-start | bytes 5898244
  116.8 14.7 %collective-permute-start.12 = (bf16[480,1792]{1,0:T(8,128)(2,1)}, bf16[480,1792]{1,0:T(8,128)(2,1)S(1)}, u32[]{:S(2)}, u32[]{:S(2)}) collective-permute-start(bf16[480,1792]{1,0:T(8,128)(2,1)} %fusion.9), channel_id=1, source_target_pairs={{0,1},{1,0},{2,3},{3,2},{4,5},{5,4},{6,7},{7,6},{8,9},{9,8},{10,11... | collective-permute-start | bytes 5160968 | tf_op jit(solution)/shard_map/ppermute | solution.py:29
  118.6 2.8 %copy-start.16 = (bf16[512,1792]{1,0:T(8,128)(2,1)S(1)}, bf16[512,1792]{1,0:T(8,128)(2,1)}, u32[]{:S(2)}) copy-start(bf16[512,1792]{1,0:T(8,128)(2,1)} %get-tuple-element.31) | copy-start | bytes 5505028
  119.2 1.5 copy-start.13
  119.2 4.8 %slice-start = ((s8[4751360]{0:T(1024)(128)(4,1)}), s8[4194304]{0:T(1024)(128)(4,1)S(1)}, s32[]{:S(2)}) async-start(s8[4751360]{0:T(1024)(128)(4,1)} %bitcast.54), calls=%async_computation | async-start | bytes 8388608
  121.4 2.5 %slice-start.1 = ((s8[4751360]{0:T(1024)(128)(4,1)}), s8[557056]{0:T(1024)(128)(4,1)S(1)}, s32[]{:S(2)}) async-start(s8[4751360]{0:T(1024)(128)(4,1)} %bitcast.54), calls=%async_computation.1 | async-start | bytes 1114112
  124.5 2.4 %collective-permute-start.19 = (f32[160]{0:T(256)S(1)}, f32[160]{0:T(256)S(1)}, u32[]{:S(2)}, u32[]{:S(2)}) collective-permute-start(f32[160]{0:T(256)S(1)} %compare_select_fusion.4), channel_id=1, source_target_pairs={{0,1},{1,0},{2,3},{3,2},{4,5},{5,4},{6,7},{7,6},{8,9},{9,8},{10,11... | collective-permute-start | bytes 1928 | tf_op jit(solution)/shard_map/ppermute | solution.py:29
  126.5 2.1 %collective-permute-start.18 = (bf16[160,1792]{1,0:T(8,128)(2,1)S(1)}, bf16[160,1792]{1,0:T(8,128)(2,1)S(1)}, u32[]{:S(2)}, u32[]{:S(2)}) collective-permute-start(bf16[160,1792]{1,0:T(8,128)(2,1)S(1)} %fusion.33), channel_id=1, source_target_pairs={{0,1},{1,0},{2,3},{3,2},{4,5},{5,4},{6,7},{7,6},{8,9},{9,8},{10,11... | collective-permute-start | bytes 1720328 | tf_op jit(solution)/shard_map/ppermute | solution.py:29
  127.0 4.6 %copy-start = (f32[480,1920]{1,0:T(8,128)S(1)}, f32[480,1920]{1,0:T(8,128)}, u32[]{:S(2)}) copy-start(f32[480,1920]{1,0:T(8,128)} %fusion.102) | copy-start | bytes 11059204
  128.8 9.1 %collective-permute-start.20 = (bf16[80,1920]{1,0:T(8,128)(2,1)S(1)}, bf16[80,1920]{1,0:T(8,128)(2,1)S(1)}, u32[]{:S(2)}, u32[]{:S(2)}) collective-permute-start(bf16[80,1920]{1,0:T(8,128)(2,1)S(1)} %get-tuple-element.46), channel_id=1, source_target_pairs={{0,6},{1,7},{2,0},{3,1},{4,2},{5,3},{6,4},{7,5},{8,14},{9,15},{10,... | collective-permute-start | bytes 921608 | tf_op jit(solution)/shard_map/ppermute | solution.py:25
  132.4 17.2 %collective-permute-start.14 = (bf16[80,1920]{1,0:T(8,128)(2,1)S(1)}, bf16[80,1920]{1,0:T(8,128)(2,1)S(1)}, u32[]{:S(2)}, u32[]{:S(2)}) collective-permute-start(bf16[80,1920]{1,0:T(8,128)(2,1)S(1)} %get-tuple-element.41), channel_id=1, source_target_pairs={{0,2},{1,3},{2,4},{3,5},{4,6},{5,7},{6,0},{7,1},{8,10},{9,11},{10,... | collective-permute-start | bytes 921608 | tf_op jit(solution)/shard_map/ppermute | solution.py:25
  132.5 15.9 %collective-permute-start.24 = (bf16[80,1920]{1,0:T(8,128)(2,1)S(1)}, bf16[80,1920]{1,0:T(8,128)(2,1)S(1)}, u32[]{:S(2)}, u32[]{:S(2)}) collective-permute-start(bf16[80,1920]{1,0:T(8,128)(2,1)S(1)} %get-tuple-element.50), channel_id=1, source_target_pairs={{0,2},{1,3},{2,4},{3,5},{4,6},{5,7},{6,0},{7,1},{8,10},{9,11},{10,... | collective-permute-start | bytes 921608 | tf_op jit(solution)/shard_map/ppermute | solution.py:25
  137.9 11.7 %collective-permute-start.21 = (bf16[80,1920]{1,0:T(8,128)(2,1)S(1)}, bf16[80,1920]{1,0:T(8,128)(2,1)S(1)}, u32[]{:S(2)}, u32[]{:S(2)}) collective-permute-start(bf16[80,1920]{1,0:T(8,128)(2,1)S(1)} %add.248), channel_id=1, source_target_pairs={{0,6},{1,7},{2,0},{3,1},{4,2},{5,3},{6,4},{7,5},{8,14},{9,15},{10,... | collective-permute-start | bytes 921608 | tf_op jit(solution)/shard_map/ppermute | solution.py:25
  148.0 10.4 %copy-start.8 = (bf16[480,512]{1,0:T(8,128)(2,1)S(1)}, bf16[480,512]{1,0:T(8,128)(2,1)}, u32[]{:S(2)}) copy-start(bf16[480,512]{1,0:T(8,128)(2,1)} %copy-done.7) | copy-start | bytes 1474564
  148.0 7.3 %collective-permute-start.23 = (bf16[80,1920]{1,0:T(8,128)(2,1)S(1)}, bf16[80,1920]{1,0:T(8,128)(2,1)S(1)}, u32[]{:S(2)}, u32[]{:S(2)}) collective-permute-start(bf16[80,1920]{1,0:T(8,128)(2,1)S(1)} %get-tuple-element.48), channel_id=1, source_target_pairs={{0,6},{1,7},{2,0},{3,1},{4,2},{5,3},{6,4},{7,5},{8,14},{9,15},{10,... | collective-permute-start | bytes 921608 | tf_op jit(solution)/shard_map/ppermute | solution.py:25
  148.5 8.5 %collective-permute-start.25 = (bf16[80,1920]{1,0:T(8,128)(2,1)S(1)}, bf16[80,1920]{1,0:T(8,128)(2,1)S(1)}, u32[]{:S(2)}, u32[]{:S(2)}) collective-permute-start(bf16[80,1920]{1,0:T(8,128)(2,1)S(1)} %add.251), channel_id=1, source_target_pairs={{0,2},{1,3},{2,4},{3,5},{4,6},{5,7},{6,0},{7,1},{8,10},{9,11},{10,... | collective-permute-start | bytes 921608 | tf_op jit(solution)/shard_map/ppermute | solution.py:25
  149.8 15.3 %collective-permute-start.22 = (bf16[40,1920]{1,0:T(8,128)(2,1)S(1)}, bf16[40,1920]{1,0:T(8,128)(2,1)S(1)}, u32[]{:S(2)}, u32[]{:S(2)}) collective-permute-start(bf16[40,1920]{1,0:T(8,128)(2,1)S(1)} %get-tuple-element.106), channel_id=1, source_target_pairs={{0,24},{8,0},{16,8},{24,16},{32,56},{40,32},{48,40},{56,48},{64,88... | collective-permute-start | bytes 460808 | tf_op jit(solution)/shard_map/ppermute | solution.py:20
  157.2 7.9 %collective-permute-start.26 = (bf16[40,1920]{1,0:T(8,128)(2,1)S(1)}, bf16[40,1920]{1,0:T(8,128)(2,1)S(1)}, u32[]{:S(2)}, u32[]{:S(2)}) collective-permute-start(bf16[40,1920]{1,0:T(8,128)(2,1)S(1)} %get-tuple-element.107), channel_id=1, source_target_pairs={{0,16},{8,24},{16,0},{24,8},{32,48},{40,56},{48,32},{56,40},{64,80... | collective-permute-start | bytes 460808 | tf_op jit(solution)/shard_map/ppermute | solution.py:20
  157.5 9.0 %collective-permute-start.27 = (bf16[40,1920]{1,0:T(8,128)(2,1)S(1)}, bf16[40,1920]{1,0:T(8,128)(2,1)S(1)}, u32[]{:S(2)}, u32[]{:S(2)}) collective-permute-start(bf16[40,1920]{1,0:T(8,128)(2,1)S(1)} %get-tuple-element.108), channel_id=1, source_target_pairs={{0,8},{8,16},{16,24},{24,0},{32,40},{40,48},{48,56},{56,32},{64,72... | collective-permute-start | bytes 460808 | tf_op jit(solution)/shard_map/ppermute | solution.py:20
  165.0 5.6 %copy-start.19 = (bf16[480,512]{1,0:T(8,128)(2,1)S(1)}, bf16[480,512]{1,0:T(8,128)(2,1)}, u32[]{:S(2)}) copy-start(bf16[480,512]{1,0:T(8,128)(2,1)} %get-tuple-element.51) | copy-start | bytes 1474564
  166.9 9.6 %collective-permute-start.28 = (bf16[32,1920]{1,0:T(8,128)(2,1)S(1)}, bf16[32,1920]{1,0:T(8,128)(2,1)S(1)}, u32[]{:S(2)}, u32[]{:S(2)}) collective-permute-start(bf16[32,1920]{1,0:T(8,128)(2,1)S(1)} %get-tuple-element.98), channel_id=1, source_target_pairs={{0,96},{8,104},{16,112},{24,120},{32,0},{40,8},{48,16},{56,24},{64... | collective-permute-start | bytes 368648 | tf_op jit(solution)/shard_map/ppermute | solution.py:15
  170.0 6.6 %collective-permute-start.30 = (bf16[32,1920]{1,0:T(8,128)(2,1)S(1)}, bf16[32,1920]{1,0:T(8,128)(2,1)S(1)}, u32[]{:S(2)}, u32[]{:S(2)}) collective-permute-start(bf16[32,1920]{1,0:T(8,128)(2,1)S(1)} %get-tuple-element.99), channel_id=1, source_target_pairs={{0,64},{8,72},{16,80},{24,88},{32,96},{40,104},{48,112},{56,120},{... | collective-permute-start | bytes 368648 | tf_op jit(solution)/shard_map/ppermute | solution.py:15
  170.1 6.4 %collective-permute-start.29 = (bf16[32,1920]{1,0:T(8,128)(2,1)S(1)}, bf16[32,1920]{1,0:T(8,128)(2,1)S(1)}, u32[]{:S(2)}, u32[]{:S(2)}) collective-permute-start(bf16[32,1920]{1,0:T(8,128)(2,1)S(1)} %get-tuple-element.100), channel_id=1, source_target_pairs={{0,32},{8,40},{16,48},{24,56},{32,64},{40,72},{48,80},{56,88},{64,... | collective-permute-start | bytes 368648 | tf_op jit(solution)/shard_map/ppermute | solution.py:15
  176.7 4.2 %collective-permute-start.31 = (bf16[16,1792]{1,0:T(8,128)(2,1)S(1)}, bf16[16,1792]{1,0:T(8,128)(2,1)S(1)}, u32[]{:S(2)}, u32[]{:S(2)}) collective-permute-start(bf16[16,1792]{1,0:T(8,128)(2,1)S(1)} %slice.150), channel_id=1, source_target_pairs={{0,1},{1,0},{2,3},{3,2},{4,5},{5,4},{6,7},{7,6},{8,9},{9,8},{10,11... | collective-permute-start | bytes 172040 | tf_op jit(solution)/shard_map/ppermute | solution.py:29
where the time goes:
time: 182 us
  waiting for transfers between devices  54.1 us (30%)
  matrix products  45.8 us (25%)
  starting transfers between devices  38.1 us (21%)
  local copies, waits for them, and re-layouts  22.3 us (12%)
  Pallas kernels  13 us (7%)
  other arithmetic  7.06 us (4%)
    dot_general x27, matrix products, dot(): lax.dot_general(left, right, ((dims[0], dims[1]), ((), ())), preferred_el...  45.8 us
    ppermute x10, waiting for transfers between devices, along_y(): return lax.ppermute(value, 'local', pairs)  35.1 us
    unnamed x57, local copies, waits for them, and re-layouts  16.4 us
    ppermute x10, starting transfers between devices, along_y(): return lax.ppermute(value, 'local', pairs)  13.9 us
    ppermute x6, waiting for transfers between devices, along_x(): return lax.ppermute(value, 'node', pairs)  9.1 us
    ppermute x10, starting transfers between devices, across(): return lax.ppermute(value, 'local', [(i, i ^ 1) for i in range(8)])  8.99 us
    ppermute x6, starting transfers between devices, along_x(): return lax.ppermute(value, 'node', pairs)  8.67 us
    pallas_call x1, Pallas kernels, per_device(): pl.pallas_call(weight_kernel, out_shape=[jax.ShapeDtypeStruct((half + TAI...  8.63 us
  transfers between devices with their start and end apart: 32, of which 12 were waited for; matrix products, arithmetic and copies ran while one was open for 36% of the time, Pallas kernels for 5%

commit v1 on v0

--- a/solution.py
+++ b/solution.py
@@ -52,6 +52,10 @@
 
 def tn(left, right):
     return dot(left, right, ((0,), (0,)))
+
+
+def limit(mebibytes):
+    return pltpu.CompilerParams(vmem_limit_bytes=mebibytes * 1024 * 1024)
 
 
 def vmem(count):
@@ -83,22 +87,22 @@
         out[:, half + TAIL :] = jnp.where(is_left, cot[:, :half], cot[:, half:])
 
 
-def weight_kernel(core, gate, up, down, _, gate_own, gate_oth, up_own, up_oth, down_own, down_oth, sems):
+def weight_kernel(core, gate, up, down, _, own, oth, down_own, down_oth, sems):
     half = down_own.shape[1]
+    hid_width = gate.shape[1]
     copies = []
-    for src, outs in ((gate, (gate_own, gate_oth)), (up, (up_own, up_oth))):
-        for out, which in zip(outs, (core[0], 1 - core[0])):
-            rows = pl.ds(pl.multiple_of(which * half, half), half)
-            copies.append((src.at[rows, :], out.at[pl.ds(0, half), :]))
-    for out, which in ((down_own, core[0]), (down_oth, 1 - core[0])):
-        cols = pl.ds(pl.multiple_of(which * half, half), half)
-        copies.append((down.at[:, cols], out))
+    for out, down_out, which in ((own, down_own, core[0]), (oth, down_oth, 1 - core[0])):
+        place = pl.ds(pl.multiple_of(which * half, half), half)
+        top = pl.ds(0, half)
+        copies.append((gate.at[place, :], out.at[top, pl.ds(0, hid_width)]))
+        copies.append((up.at[place, :], out.at[top, pl.ds(hid_width, hid_width)]))
+        copies.append((down.at[:, place], down_out))
     copies = [
         pltpu.make_async_copy(src, dst, sems.at[i]) for i, (src, dst) in enumerate(copies)
     ]
     for copy in copies:
         copy.start()
-    for out in (gate_own, gate_oth, up_own, up_oth):
+    for out in (own, oth):
         out[half:, :] = jnp.zeros((out.shape[0] - half, out.shape[1]), BF)
     for copy in copies:
         copy.wait()
@@ -132,6 +136,7 @@
         out_shape=[jax.ShapeDtypeStruct((tok, width + TAIL), BF)] * 2,
         in_specs=[pl.BlockSpec(memory_space=pltpu.SMEM)] + [pl.BlockSpec()] * 6,
         out_specs=vmem(2),
+        compiler_params=limit(4),
     )(
         core_arg,
         tokens,
@@ -168,15 +173,16 @@
     side = 2 * slots
 
     hid_width = gate_w.shape[2]
-    gate_own, gate_oth, up_own, up_oth, down_own, down_oth = pl.pallas_call(
+    proj_own, proj_oth, down_own, down_oth = pl.pallas_call(
         weight_kernel,
-        out_shape=[jax.ShapeDtypeStruct((half + TAIL, hid_width), BF)] * 4
+        out_shape=[jax.ShapeDtypeStruct((half + TAIL, 2 * hid_width), BF)] * 2
         + [jax.ShapeDtypeStruct((hid_width, half), BF)] * 2,
         in_specs=[pl.BlockSpec(memory_space=pltpu.SMEM)]
         + [pl.BlockSpec(memory_space=pltpu.HBM)] * 3
         + [anywhere],
-        out_specs=vmem(6),
+        out_specs=vmem(4),
         scratch_shapes=[pltpu.SemaphoreType.DMA((6,))],
+        compiler_params=limit(14),
     )(core_arg, gate_w[0], up_w[0], down_w[0], raw_send)
 
     mine = jnp.concatenate(exchange_z(parts, 1), axis=0)
@@ -193,8 +199,8 @@
             axis=1,
             keepdims=True,
         )
-        pre_gate = nn(x_own, gate_own) + nn(x_oth, gate_oth)
-        pre_up = nn(x_own, up_own) + nn(x_oth, up_oth)
+        pre = nn(x_own, proj_own) + nn(x_oth, proj_oth)
+        pre_gate, pre_up = pre[:, :hid_width], pre[:, hid_width:]
         activated, slope = silu_parts(pre_gate)
         hidden = (activated * pre_up).astype(BF)
         scaled = (weight * hidden.astype(F32)).astype(BF)
@@ -202,37 +208,41 @@
             (hidden, scaled, weight * (pre_up * slope), weight * activated)
         )
         hidden_grad = nt(d_own, down_own) + nt(d_oth, down_oth)
-        gate_grad = (hidden_grad * for_gate).astype(BF)
-        up_grad = (hidden_grad * for_up).astype(BF)
-        got = across((nt(gate_grad, gate_oth) + nt(up_grad, up_oth)).astype(BF)[:, :half])
-        keep = nt(gate_grad, gate_own) + nt(up_grad, up_own)
+        grads = jnp.concatenate(
+            [(hidden_grad * for_gate).astype(BF), (hidden_grad * for_up).astype(BF)], axis=1
+        )
+        got = across(nt(grads, proj_oth[:half]).astype(BF))
+        keep = nt(grads, proj_own[:half])
         router = jnp.sum(hidden_grad * hidden.astype(F32), axis=1)
         router = jnp.where(weight[:, 0] != 0, router, 0.0)
         router = (router + across(router))[:, None]
         high = router.astype(BF).astype(F32)
         tail = jnp.where(tail_lane == my_expert, high, 0.0)
         tail = jnp.where(tail_lane == my_expert + TAIL // 2, router - high, tail).astype(BF)
-        full = (keep[:, :half] + got.astype(F32)).astype(BF)
-        full = jnp.concatenate([full, tail], axis=1)
-        pieces = lax.optimization_barrier(tuple(jnp.split(full, own.shape[0] // side, axis=0)))
-        return (own, oth, gate_grad, up_grad, scaled), pieces
-
-    near_state, pieces = row_gradients(
+        full = jnp.concatenate([(keep + got.astype(F32)).astype(BF), tail], axis=1)
+        return (own, oth, grads, scaled), full
+
+    near_state, near_full = row_gradients(
         jnp.concatenate(near, axis=0), jnp.concatenate([across(p) for p in near], axis=0)
     )
-    own_top, own_bottom, below_top, below_bottom, above_top, above_bottom = pieces
     far = pl.pallas_call(
         stack_kernel,
         out_shape=jax.ShapeDtypeStruct((2 * side, rows.shape[1]), BF),
         in_specs=vmem(3),
         out_specs=vmem(1)[0],
+        compiler_params=limit(4),
     )(*far_parts, near_state[2])
-    far_state, (far_top, far_bottom) = row_gradients(far, across(far))
-    from_above = along_y(far_top, -1)
-    from_below = along_y(far_bottom, 1)
-    early_top, early_bottom = along_y(above_top, 1), along_y(below_bottom, -1)
-    late_top = along_y(below_top + from_above, -1)
-    late_bottom = along_y(above_bottom + from_below, 1)
+    far_state, far_full = row_gradients(far, across(far))
+
+    near_full, far_full = lax.optimization_barrier((near_full, far_full))
+    own_top, own_bottom, below_top, below_bottom, above_top, above_bottom = jnp.split(
+        near_full, 6, axis=0
+    )
+    from_above = along_y(jnp.concatenate([far_full[:side], below_bottom], axis=0), -1)
+    from_below = along_y(jnp.concatenate([far_full[side:], above_top], axis=0), 1)
+    early_top, early_bottom = from_below[side:], from_above[side:]
+    late_top = along_y(below_top + from_above[:side], -1)
+    late_bottom = along_y(above_bottom + from_below[:side], 1)
 
     def add(*parts):
         return sum(p.astype(F32) for p in parts).astype(BF)
@@ -260,7 +270,7 @@
     onehot = ids[:, :, None] == jnp.arange(TAIL, dtype=jnp.int32)[None, None, :]
     d_gates = jnp.sum(jnp.where(onehot, by_expert[:, None, :], 0.0), axis=2).astype(BF)
 
-    own, oth, gate_grad, up_grad, scaled = [
+    own, oth, grads, scaled = [
         jnp.concatenate(both, axis=0)
         for both in zip(near_state, far_state)
     ]
@@ -277,8 +287,8 @@
     return (
         d_tokens,
         d_gates,
-        tn(x_all, gate_grad).astype(BF)[None],
-        tn(x_all, up_grad).astype(BF)[None],
+        tn(x_all, grads[:, :hid_width]).astype(BF)[None],
+        tn(x_all, grads[:, hid_width:]).astype(BF)[None],
         tn(scaled, d_all).astype(BF)[None],
     )
 

time: 182 us -> 162 us (0.89)
  Pallas kernels: 13 us -> 1.78 us
  matrix products: 45.8 us -> 37.7 us
  local copies, waits for them, and re-layouts: 22.3 us -> 17.7 us
  waiting for transfers between devices: 54.1 us -> 58 us
    dot_general x27 -> x19, matrix products: 45.8 us -> 37.7 us  [dot(): lax.dot_general(left, right, ((dims[0], dims[1]), ((), ())), preferred_el...]
    pallas_call x1, Pallas kernels: 8.63 us -> 1.5 us  [per_device(): pl.pallas_call(weight_kernel, out_shape=[jax.ShapeDtypeStruct((half + TAI...]
    ppermute x10 -> x8, waiting for transfers between devices: 35.1 us -> 41.1 us  [along_y(): return lax.ppermute(value, 'local', pairs)]
    ppermute x10, starting transfers between devices: 8.99 us -> 12.3 us  [across(): return lax.ppermute(value, 'local', [(i, i ^ 1) for i in range(8)])]
    slice x2, local copies, waits for them, and re-layouts: 3.08 us -> 0.59 us  [per_device(): d_all = whole(own[:, half + TAIL:], oth[:, half + TAIL:])]
    convert_element_type x4 -> x0, other arithmetic: 2.41 us -> none  [the longest x2 1.6 us: row_gradients(): (nt(gate_grad, gate_oth) + nt(up_grad, up_oth)).astype(BF)[:, :half]]
    pallas_call x1, Pallas kernels: 2.48 us -> 0.08 us  [per_device(): pl.pallas_call(stack_kernel, out_shape=jax.ShapeDtypeStruct((2 * side, ro...]
    ppermute x10 -> x8, starting transfers between devices: 13.9 us -> 11.6 us  [along_y(): return lax.ppermute(value, 'local', pairs)]
  transfers between devices with their start and end apart: 32 -> 30, of which waited for: 12 -> 9; matrix products, arithmetic and copies ran while one was open for 36% -> 27% of each run, Pallas kernels for 5% -> 1%
where the time goes in v1:
time: 162 us; the launch traced here: 161 us
  waiting for transfers between devices  58 us (36%)
  starting transfers between devices  39.1 us (24%)
  matrix products  37.7 us (23%)
  local copies, waits for them, and re-layouts  17.7 us (11%)
  other arithmetic  5.76 us (4%)
  Pallas kernels  1.78 us (1%)
    ppermute x8, waiting for transfers between devices, along_y(): return lax.ppermute(value, 'local', pairs)  41.1 us
    dot_general x19, matrix products, dot(): lax.dot_general(left, right, ((dims[0], dims[1]), ((), ())), preferred_el...  37.7 us
    unnamed x39, local copies, waits for them, and re-layouts  16.4 us
    ppermute x10, starting transfers between devices, across(): return lax.ppermute(value, 'local', [(i, i ^ 1) for i in range(8)])  12.3 us
    ppermute x8, starting transfers between devices, along_y(): return lax.ppermute(value, 'local', pairs)  11.6 us
    ppermute x6, waiting for transfers between devices, along_x(): return lax.ppermute(value, 'node', pairs)  9.08 us
    ppermute x6, starting transfers between devices, along_x(): return lax.ppermute(value, 'node', pairs)  8.68 us
    ppermute x6, waiting for transfers between devices, along_z(): return lax.ppermute(value, 'node', pairs)  7.76 us
  transfers between devices with their start and end apart: 30, of which 9 were waited for; matrix products, arithmetic and copies ran while one was open for 27% of the time, Pallas kernels for 1%

profile of v1, /device:TPU:1, one launch (start us, length us, event | category | flops | bytes accessed | tf_op | source)
XLA Modules:
  0.0 161.2 jit_solution(14400144655592533166)
XLA Ops:
  0.7 0.9 copy-done.3
  1.5 0.9 copy-done.4
  2.4 0.7 copy-done.5
  3.1 0.7 copy-done.6
  3.8 0.7 copy-done.7
  4.5 0.7 copy-done.8
  5.3 1.5 collective-permute-start
  6.8 0.7 broadcast_multiply_fusion.2
  7.6 0.9 select_reduce_fusion.3
  8.5 1.4 collective-permute-start.1
  10.0 0.7 fusion.75
  10.7 2.5 %collective-permute-start.3 = (bf16[32,3712]{1,0:T(8,128)(2,1)S(1)}, bf16[32,3712]{1,0:T(8,128)(2,1)S(1)}, u32[]{:S(2)}, u32[]{:S(2)}) collective-permute-start(bf16[32,3712]{1,0:T(8,128)(2,1)S(1)} %get-tuple-element.105), channel_id=1, source_target_pairs={{0,64},{8,72},{16,80},{24,88},{32,96},{40,104},{48,112},{56,120},{... | collective-permute-start | bytes 712712 | tf_op jit(solution)/shard_map/ppermute | solution.py:15
  13.1 1.2 collective-permute-start.2
  14.3 2.9 %collective-permute-done.1 = bf16[32,3712]{1,0:T(8,128)(2,1)S(1)} collective-permute-done((bf16[32,3712]{1,0:T(8,128)(2,1)S(1)}, bf16[32,3712]{1,0:T(8,128)(2,1)S(1)}, u32[]{:S(2)}, u32[]{:S(2)}) %collective-permute-start.1) | collective-permute-done | bytes 237600 | tf_op jit(solution)/shard_map/ppermute | solution.py:15
  17.2 6.2 %collective-permute-done.2 = bf16[32,3712]{1,0:T(8,128)(2,1)S(1)} collective-permute-done((bf16[32,3712]{1,0:T(8,128)(2,1)S(1)}, bf16[32,3712]{1,0:T(8,128)(2,1)S(1)}, u32[]{:S(2)}, u32[]{:S(2)}) %collective-permute-start.2) | collective-permute-done | bytes 237600 | tf_op jit(solution)/shard_map/ppermute | solution.py:15
  24.0 0.5 convolution_convert_fusion.3
  24.5 0.9 constant_dynamic-update-slice_fusion.22
  25.4 3.8 %collective-permute-start.6 = (bf16[40,3712]{1,0:T(8,128)(2,1)S(1)}, bf16[40,3712]{1,0:T(8,128)(2,1)S(1)}, u32[]{:S(2)}, u32[]{:S(2)}) collective-permute-start(bf16[40,3712]{1,0:T(8,128)(2,1)S(1)} %get-tuple-element.68), channel_id=1, source_target_pairs={{0,24},{8,0},{16,8},{24,16},{32,56},{40,32},{48,40},{56,48},{64,88... | collective-permute-start | bytes 890888 | tf_op jit(solution)/shard_map/ppermute | solution.py:20
  29.3 0.7 collective-permute-start.4
  30.1 2.0 %copy-done = bf16[1,3584,512]{2,1,0:T(8,128)(2,1)S(1)} copy-done((bf16[1,3584,512]{2,1,0:T(8,128)(2,1)S(1)}, bf16[1,3584,512]{2,1,0:T(8,128)(2,1)}, u32[]{:S(2)}) %copy-start) | copy-done | bytes 3670040
  32.1 2.0 %copy-done.1 = bf16[1,3584,512]{2,1,0:T(8,128)(2,1)S(1)} copy-done((bf16[1,3584,512]{2,1,0:T(8,128)(2,1)S(1)}, bf16[1,3584,512]{2,1,0:T(8,128)(2,1)}, u32[]{:S(2)}) %copy-start.1) | copy-done | bytes 3670040
  34.1 2.0 %copy-done.2 = bf16[1,512,3584]{2,1,0:T(8,128)(2,1)S(1)} copy-done((bf16[1,512,3584]{2,1,0:T(8,128)(2,1)S(1)}, bf16[1,512,3584]{2,1,0:T(8,128)(2,1)}, u32[]{:S(2)}) %copy-start.2) | copy-done | bytes 3670040
  36.2 1.5 shard_map.129
  37.7 3.0 %collective-permute-done.6 = bf16[40,3712]{1,0:T(8,128)(2,1)S(1)} collective-permute-done((bf16[40,3712]{1,0:T(8,128)(2,1)S(1)}, bf16[40,3712]{1,0:T(8,128)(2,1)S(1)}, u32[]{:S(2)}, u32[]{:S(2)}) %collective-permute-start.6) | collective-permute-done | bytes 296992 | tf_op jit(solution)/shard_map/ppermute | solution.py:20
  40.7 4.7 %collective-permute-done.4 = bf16[40,3712]{1,0:T(8,128)(2,1)S(1)} collective-permute-done((bf16[40,3712]{1,0:T(8,128)(2,1)S(1)}, bf16[40,3712]{1,0:T(8,128)(2,1)S(1)}, u32[]{:S(2)}, u32[]{:S(2)}) %collective-permute-start.4) | collective-permute-done | bytes 296992 | tf_op jit(solution)/shard_map/ppermute | solution.py:20
  45.5 0.9 collective-permute-start.9
  46.5 2.7 %collective-permute-start.8 = (bf16[160,3712]{1,0:T(8,128)(2,1)S(1)}, bf16[160,3712]{1,0:T(8,128)(2,1)S(1)}, u32[]{:S(2)}, u32[]{:S(2)}) collective-permute-start(bf16[160,3712]{1,0:T(8,128)(2,1)S(1)} %pad_maximum_fusion.1), channel_id=1, source_target_pairs={{0,6},{1,7},{2,0},{3,1},{4,2},{5,3},{6,4},{7,5},{8,14},{9,15},{10,... | collective-permute-start | bytes 3563528 | tf_op jit(solution)/shard_map/ppermute | solution.py:25
  49.4 25.3 %collective-permute-done.8 = bf16[160,3712]{1,0:T(8,128)(2,1)S(1)} collective-permute-done((bf16[160,3712]{1,0:T(8,128)(2,1)S(1)}, bf16[160,3712]{1,0:T(8,128)(2,1)S(1)}, u32[]{:S(2)}, u32[]{:S(2)}) %collective-permute-start.8) | collective-permute-done | bytes 1187872 | tf_op jit(solution)/shard_map/ppermute | solution.py:25
  74.8 3.5 %collective-permute-start.15 = (bf16[80,3712]{1,0:T(8,128)(2,1)S(1)}, bf16[80,3712]{1,0:T(8,128)(2,1)S(1)}, u32[]{:S(2)}, u32[]{:S(2)}) collective-permute-start(bf16[80,3712]{1,0:T(8,128)(2,1)S(1)} %slice.175), channel_id=1, source_target_pairs={{0,6},{1,7},{2,0},{3,1},{4,2},{5,3},{6,4},{7,5},{8,14},{9,15},{10,... | collective-permute-start | bytes 1781768 | tf_op jit(solution)/shard_map/ppermute | solution.py:25
  78.4 1.2 collective-permute-start.11
  80.5 1.1 fusion.31
  81.6 0.7 copy-done.11
  82.5 1.8 %copy-done.12 = bf16[480,3712]{1,0:T(8,128)(2,1)S(1)} copy-done((bf16[480,3712]{1,0:T(8,128)(2,1)S(1)}, bf16[480,3712]{1,0:T(8,128)(2,1)}, u32[]{:S(2)}) %copy-start.12) | copy-done | bytes 3563544
  84.5 2.3 %fusion.27 = f32[480,1024]{1,0:T(8,128)S(1)} fusion(bf16[1920,1024]{1,0:T(8,128)(2,1)S(1)} %get-tuple-element.25, bf16[480,3712]{1,0:T(8,128)(2,1)S(1)} %copy-done.12), kind=kOutput, calls=%fused_computation.29 | convolution fusion | flops 1887436800 | bytes 7741440 | tf_op jit(solution)/shard_map/dot_general | solution.py:33
  87.4 2.3 %fusion.33 = f32[480,1024]{1,0:T(8,128)S(1)} fusion(f32[480,1024]{1,0:T(8,128)S(1)} %fusion.27, bf16[1920,1024]{1,0:T(8,128)(2,1)S(1)} %get-tuple-element.26, bf16[480,3712]{1,0:T(8,128)(2,1)S(1)} %get-tuple-element.73), kind=kOutput, calls=%fused_computation.36 | convolution fusion | flops 1887928320 | bytes 9707520 | tf_op jit(solution)/shard_map/dot_general | solution.py:33
  89.7 0.6 broadcast_multiply_fusion
  90.3 1.3 multiply_convert_fusion.1
  91.6 0.3 collective-permute-start.13
  92.0 1.3 collective-permute-done.14.top
  93.4 2.1 %collective-permute-start.16 = (bf16[160,3712]{1,0:T(8,128)(2,1)S(1)}, bf16[160,3712]{1,0:T(8,128)(2,1)S(1)}, u32[]{:S(2)}, u32[]{:S(2)}) collective-permute-start(bf16[160,3712]{1,0:T(8,128)(2,1)S(1)} %shard_map.130), channel_id=1, source_target_pairs={{0,1},{1,0},{2,3},{3,2},{4,5},{5,4},{6,7},{7,6},{8,9},{9,8},{10,11... | collective-permute-start | bytes 3563528 | tf_op jit(solution)/shard_map/ppermute | solution.py:29
  96.0 2.0 %fusion.17 = bf16[480,1792]{1,0:T(8,128)(2,1)S(1)} fusion(bf16[1920,1024]{1,0:T(8,128)(2,1)S(1)} %get-tuple-element.26, bf16[480,512]{1,0:T(8,128)(2,1)S(1)} %get-tuple-element.80, bf16[480,512]{1,0:T(8,128)(2,1)S(1)} %get-tuple-element.78), kind=kOutput, calls=%fused_computation.24 | convolution fusion | flops 1764433920 | bytes 6373376 | tf_op jit(solution)/shard_map/dot_general | solution.py:33
  98.5 0.9 fusion.47
  99.4 0.9 convolution_add_fusion
  100.5 0.7 fusion.57
  101.2 0.9 multiply_convert_fusion.5
  102.1 0.8 collective-permute-start.18
  102.9 1.3 fusion.22
  104.8 2.0 %add_convert_fusion = bf16[480,1792]{1,0:T(8,128)(2,1)S(1)} fusion(bf16[480,1792]{1,0:T(8,128)(2,1)S(1)} %collective-permute-done.12, bf16[1920,1024]{1,0:T(8,128)(2,1)S(1)} %get-tuple-element.25, bf16[480,512]{1,0:T(8,128)(2,1)S(1)} %get-tuple-element.80, bf16[480,512]{1,0:T(8,128)(2,1)S(1)} %get-tuple-element.78), kind=kOutput, calls=%fused_computation.15 | convolution fusion | flops 1766154240 | bytes 8093696 | tf_op jit(solution)/shard_map/dot_general | solution.py:33
  107.0 1.4 add_convert_fusion.1
  108.7 2.7 %collective-permute-start.20 = (bf16[160,1920]{1,0:T(8,128)(2,1)S(1)}, bf16[160,1920]{1,0:T(8,128)(2,1)S(1)}, u32[]{:S(2)}, u32[]{:S(2)}) collective-permute-start(bf16[160,1920]{1,0:T(8,128)(2,1)S(1)} %pad_maximum_fusion.5), channel_id=1, source_target_pairs={{0,6},{1,7},{2,0},{3,1},{4,2},{5,3},{6,4},{7,5},{8,14},{9,15},{10,... | collective-permute-start | bytes 1843208 | tf_op jit(solution)/shard_map/ppermute | solution.py:25
  111.7 13.1 %collective-permute-done.19 = bf16[160,1920]{1,0:T(8,128)(2,1)S(1)} collective-permute-done((bf16[160,1920]{1,0:T(8,128)(2,1)S(1)}, bf16[160,1920]{1,0:T(8,128)(2,1)S(1)}, u32[]{:S(2)}, u32[]{:S(2)}) %collective-permute-start.19) | collective-permute-done | bytes 614432 | tf_op jit(solution)/shard_map/ppermute | solution.py:25
  124.9 2.5 %collective-permute-start.21 = (bf16[80,1920]{1,0:T(8,128)(2,1)S(1)}, bf16[80,1920]{1,0:T(8,128)(2,1)S(1)}, u32[]{:S(2)}, u32[]{:S(2)}) collective-permute-start(bf16[80,1920]{1,0:T(8,128)(2,1)S(1)} %get-tuple-element.58), channel_id=1, source_target_pairs={{0,6},{1,7},{2,0},{3,1},{4,2},{5,3},{6,4},{7,5},{8,14},{9,15},{10,... | collective-permute-start | bytes 921608 | tf_op jit(solution)/shard_map/ppermute | solution.py:25
  127.4 6.7 %fusion.1 = bf16[1,3584,512]{2,1,0:T(8,128)(2,1)} fusion(bf16[640,1792]{1,0:T(8,128)(2,1)S(1)} %get-tuple-element.51, bf16[640,1792]{1,0:T(8,128)(2,1)S(1)} %get-tuple-element.49, pred[]{:T(512)S(6)} %eq.114, bf16[640,1024]{1,0:T(8,128)(2,1)S(1)} %maximum_maximum_fusion), kind=kOutput, calls=%fused_computation.4 | convolution fusion | flops 2371289088 | bytes 8912897 | tf_op jit(solution)/shard_map/dot_general | solution.py:33
  134.1 1.4 collective-permute-done.23
  135.8 0.7 collective-permute-start.22
  136.6 1.2 collective-permute-start.25
  137.8 6.7 %fusion = bf16[1,3584,512]{2,1,0:T(8,128)(2,1)} fusion(bf16[640,1792]{1,0:T(8,128)(2,1)S(1)} %get-tuple-element.51, bf16[640,1792]{1,0:T(8,128)(2,1)S(1)} %get-tuple-element.49, pred[]{:T(512)S(6)} %eq.114, bf16[640,1024]{1,0:T(8,128)(2,1)S(1)} %maximum_maximum_fusion), kind=kOutput, calls=%fused_computation.3 | convolution fusion | flops 2371289088 | bytes 8912897 | tf_op jit(solution)/shard_map/dot_general | solution.py:33
  144.5 0.4 convolution_convert_fusion.4
  144.9 3.0 %collective-permute-start.26 = (bf16[32,1920]{1,0:T(8,128)(2,1)S(1)}, bf16[32,1920]{1,0:T(8,128)(2,1)S(1)}, u32[]{:S(2)}, u32[]{:S(2)}) collective-permute-start(bf16[32,1920]{1,0:T(8,128)(2,1)S(1)} %get-tuple-element.87), channel_id=1, source_target_pairs={{0,96},{8,104},{16,112},{24,120},{32,0},{40,8},{48,16},{56,24},{64... | collective-permute-start | bytes 368648 | tf_op jit(solution)/shard_map/ppermute | solution.py:15
  148.1 0.5 collective-permute-start.27
  148.6 6.0 %fusion.2 = bf16[1,512,3584]{2,1,0:T(8,128)(2,1)} fusion(bf16[640,1792]{1,0:T(8,128)(2,1)S(1)} %get-tuple-element.50, bf16[640,1792]{1,0:T(8,128)(2,1)S(1)} %get-tuple-element.48, pred[]{:T(512)S(6)} %eq.114, bf16[160,512]{1,0:T(8,128)(2,1)S(1)} %get-tuple-element.36, bf16[480,512]{1,0:T(8,128)(2,1)S(1)} %get-tuple-element.35), kind=kOutput, calls=%fused_computation.5 | convolution fusion | flops 2372599808 | bytes 8912897 | tf_op jit(solution)/shard_map/dot_general | solution.py:33
  154.7 4.9 %collective-permute-start.29 = (bf16[16,1792]{1,0:T(8,128)(2,1)S(1)}, bf16[16,1792]{1,0:T(8,128)(2,1)S(1)}, u32[]{:S(2)}, u32[]{:S(2)}) collective-permute-start(bf16[16,1792]{1,0:T(8,128)(2,1)S(1)} %slice.192), channel_id=1, source_target_pairs={{0,1},{1,0},{2,3},{3,2},{4,5},{5,4},{6,7},{7,6},{8,9},{9,8},{10,11... | collective-permute-start | bytes 172040 | tf_op jit(solution)/shard_map/ppermute | solution.py:29
  159.8 0.7 copy.19
  160.6 0.7 pad_maximum_fusion.11
  (112 shorter events, 7.0 us)
Async XLA Ops:
  0.6 0.9 copy-start.3
  1.5 0.9 copy-start.4
  2.4 0.7 copy-start.5
  3.1 0.7 copy-start.6
  3.8 0.7 copy-start.7
  4.5 0.7 copy-start.8
  5.3 3.1 %collective-permute-start = (bf16[16,3712]{1,0:T(8,128)(2,1)S(1)}, bf16[16,3712]{1,0:T(8,128)(2,1)S(1)}, u32[]{:S(2)}, u32[]{:S(2)}) collective-permute-start(bf16[16,3712]{1,0:T(8,128)(2,1)S(1)} %get-tuple-element.22._), channel_id=1, source_target_pairs={{0,1},{1,0},{2,3},{3,2},{4,5},{5,4},{6,7},{7,6},{8,9},{9,8},{10,11... | collective-permute-start | bytes 356360 | tf_op jit(solution)/shard_map/ppermute | solution.py:29
  8.5 8.7 %collective-permute-start.1 = (bf16[32,3712]{1,0:T(8,128)(2,1)S(1)}, bf16[32,3712]{1,0:T(8,128)(2,1)S(1)}, u32[]{:S(2)}, u32[]{:S(2)}) collective-permute-start(bf16[32,3712]{1,0:T(8,128)(2,1)S(1)} %get-tuple-element.105), channel_id=1, source_target_pairs={{0,32},{8,40},{16,48},{24,56},{32,64},{40,72},{48,80},{56,88},{64,... | collective-permute-start | bytes 712712 | tf_op jit(solution)/shard_map/ppermute | solution.py:15
  10.7 12.7 %collective-permute-start.3 = (bf16[32,3712]{1,0:T(8,128)(2,1)S(1)}, bf16[32,3712]{1,0:T(8,128)(2,1)S(1)}, u32[]{:S(2)}, u32[]{:S(2)}) collective-permute-start(bf16[32,3712]{1,0:T(8,128)(2,1)S(1)} %get-tuple-element.105), channel_id=1, source_target_pairs={{0,64},{8,72},{16,80},{24,88},{32,96},{40,104},{48,112},{56,120},{... | collective-permute-start | bytes 712712 | tf_op jit(solution)/shard_map/ppermute | solution.py:15
  13.1 10.3 %collective-permute-start.2 = (bf16[32,3712]{1,0:T(8,128)(2,1)S(1)}, bf16[32,3712]{1,0:T(8,128)(2,1)S(1)}, u32[]{:S(2)}, u32[]{:S(2)}) collective-permute-start(bf16[32,3712]{1,0:T(8,128)(2,1)S(1)} %get-tuple-element.105), channel_id=1, source_target_pairs={{0,96},{8,104},{16,112},{24,120},{32,0},{40,8},{48,16},{56,24},{64... | collective-permute-start | bytes 712712 | tf_op jit(solution)/shard_map/ppermute | solution.py:15
  25.4 15.3 %collective-permute-start.6 = (bf16[40,3712]{1,0:T(8,128)(2,1)S(1)}, bf16[40,3712]{1,0:T(8,128)(2,1)S(1)}, u32[]{:S(2)}, u32[]{:S(2)}) collective-permute-start(bf16[40,3712]{1,0:T(8,128)(2,1)S(1)} %get-tuple-element.68), channel_id=1, source_target_pairs={{0,24},{8,0},{16,8},{24,16},{32,56},{40,32},{48,40},{56,48},{64,88... | collective-permute-start | bytes 890888 | tf_op jit(solution)/shard_map/ppermute | solution.py:20
  29.3 11.5 %collective-permute-start.5 = (bf16[40,3712]{1,0:T(8,128)(2,1)S(1)}, bf16[40,3712]{1,0:T(8,128)(2,1)S(1)}, u32[]{:S(2)}, u32[]{:S(2)}) collective-permute-start(bf16[40,3712]{1,0:T(8,128)(2,1)S(1)} %get-tuple-element.69), channel_id=1, source_target_pairs={{0,16},{8,24},{16,0},{24,8},{32,48},{40,56},{48,32},{56,40},{64,80... | collective-permute-start | bytes 890888 | tf_op jit(solution)/shard_map/ppermute | solution.py:20
  29.3 16.2 %collective-permute-start.4 = (bf16[40,3712]{1,0:T(8,128)(2,1)S(1)}, bf16[40,3712]{1,0:T(8,128)(2,1)S(1)}, u32[]{:S(2)}, u32[]{:S(2)}) collective-permute-start(bf16[40,3712]{1,0:T(8,128)(2,1)S(1)} %get-tuple-element.70), channel_id=1, source_target_pairs={{0,8},{8,16},{16,24},{24,0},{32,40},{40,48},{48,56},{56,32},{64,72... | collective-permute-start | bytes 890888 | tf_op jit(solution)/shard_map/ppermute | solution.py:20
  30.1 2.0 %copy-start = (bf16[1,3584,512]{2,1,0:T(8,128)(2,1)S(1)}, bf16[1,3584,512]{2,1,0:T(8,128)(2,1)}, u32[]{:S(2)}) copy-start(bf16[1,3584,512]{2,1,0:T(8,128)(2,1)} %param.15) | copy-start | bytes 11010052
  32.1 2.0 %copy-start.1 = (bf16[1,3584,512]{2,1,0:T(8,128)(2,1)S(1)}, bf16[1,3584,512]{2,1,0:T(8,128)(2,1)}, u32[]{:S(2)}) copy-start(bf16[1,3584,512]{2,1,0:T(8,128)(2,1)} %param.16) | copy-start | bytes 11010052
  34.1 2.0 %copy-start.2 = (bf16[1,512,3584]{2,1,0:T(8,128)(2,1)S(1)}, bf16[1,512,3584]{2,1,0:T(8,128)(2,1)}, u32[]{:S(2)}) copy-start(bf16[1,512,3584]{2,1,0:T(8,128)(2,1)} %param.17) | copy-start | bytes 11010052
  36.2 13.1 %copy-start.9 = (bf16[640,3712]{1,0:T(8,128)(2,1)S(1)}, bf16[640,3712]{1,0:T(8,128)(2,1)}, u32[]{:S(2)}) copy-start(bf16[640,3712]{1,0:T(8,128)(2,1)} %get-tuple-element.66) | copy-start | bytes 14254084
  36.2 13.1 %copy-start.10 = (bf16[480,3712]{1,0:T(8,128)(2,1)S(1)}, bf16[480,3712]{1,0:T(8,128)(2,1)}, u32[]{:S(2)}) copy-start(bf16[480,3712]{1,0:T(8,128)(2,1)} %get-tuple-element.67) | copy-start | bytes 10690564
  45.5 36.8 %collective-permute-start.9 = (bf16[160,3712]{1,0:T(8,128)(2,1)S(1)}, bf16[160,3712]{1,0:T(8,128)(2,1)S(1)}, u32[]{:S(2)}, u32[]{:S(2)}) collective-permute-start(bf16[160,3712]{1,0:T(8,128)(2,1)S(1)} %pad_maximum_fusion.1), channel_id=1, source_target_pairs={{0,1},{1,0},{2,3},{3,2},{4,5},{5,4},{6,7},{7,6},{8,9},{9,8},{10,11... | collective-permute-start | bytes 3563528 | tf_op jit(solution)/shard_map/ppermute | solution.py:29
  46.5 28.2 %collective-permute-start.8 = (bf16[160,3712]{1,0:T(8,128)(2,1)S(1)}, bf16[160,3712]{1,0:T(8,128)(2,1)S(1)}, u32[]{:S(2)}, u32[]{:S(2)}) collective-permute-start(bf16[160,3712]{1,0:T(8,128)(2,1)S(1)} %pad_maximum_fusion.1), channel_id=1, source_target_pairs={{0,6},{1,7},{2,0},{3,1},{4,2},{5,3},{6,4},{7,5},{8,14},{9,15},{10,... | collective-permute-start | bytes 3563528 | tf_op jit(solution)/shard_map/ppermute | solution.py:25
  49.2 29.0 %collective-permute-start.7 = (bf16[160,3712]{1,0:T(8,128)(2,1)S(1)}, bf16[160,3712]{1,0:T(8,128)(2,1)S(1)}, u32[]{:S(2)}, u32[]{:S(2)}) collective-permute-start(bf16[160,3712]{1,0:T(8,128)(2,1)S(1)} %pad_maximum_fusion.1), channel_id=1, source_target_pairs={{0,2},{1,3},{2,4},{3,5},{4,6},{5,7},{6,0},{7,1},{8,10},{9,11},{10,... | collective-permute-start | bytes 3563528 | tf_op jit(solution)/shard_map/ppermute | solution.py:25
  74.8 17.3 %collective-permute-start.15 = (bf16[80,3712]{1,0:T(8,128)(2,1)S(1)}, bf16[80,3712]{1,0:T(8,128)(2,1)S(1)}, u32[]{:S(2)}, u32[]{:S(2)}) collective-permute-start(bf16[80,3712]{1,0:T(8,128)(2,1)S(1)} %slice.175), channel_id=1, source_target_pairs={{0,6},{1,7},{2,0},{3,1},{4,2},{5,3},{6,4},{7,5},{8,14},{9,15},{10,... | collective-permute-start | bytes 1781768 | tf_op jit(solution)/shard_map/ppermute | solution.py:25
  78.3 15.0 %collective-permute-start.14 = (bf16[80,3712]{1,0:T(8,128)(2,1)S(1)}, bf16[80,3712]{1,0:T(8,128)(2,1)S(1)}, u32[]{:S(2)}, u32[]{:S(2)}) collective-permute-start(bf16[80,3712]{1,0:T(8,128)(2,1)S(1)} %slice.174), channel_id=1, source_target_pairs={{0,2},{1,3},{2,4},{3,5},{4,6},{5,7},{6,0},{7,1},{8,10},{9,11},{10,... | collective-permute-start | bytes 1781768 | tf_op jit(solution)/shard_map/ppermute | solution.py:25
  78.4 8.7 %collective-permute-start.11 = (bf16[160,3712]{1,0:T(8,128)(2,1)S(1)}, bf16[160,3712]{1,0:T(8,128)(2,1)S(1)}, u32[]{:S(2)}, u32[]{:S(2)}) collective-permute-start(bf16[160,3712]{1,0:T(8,128)(2,1)S(1)} %collective-permute-done.8), channel_id=1, source_target_pairs={{0,1},{1,0},{2,3},{3,2},{4,5},{5,4},{6,7},{7,6},{8,9},{9,8},{10,11... | collective-permute-start | bytes 3563528 | tf_op jit(solution)/shard_map/ppermute | solution.py:29
  79.6 7.1 %collective-permute-start.10 = (bf16[160,3712]{1,0:T(8,128)(2,1)S(1)}, bf16[160,3712]{1,0:T(8,128)(2,1)S(1)}, u32[]{:S(2)}, u32[]{:S(2)}) collective-permute-start(bf16[160,3712]{1,0:T(8,128)(2,1)S(1)} %collective-permute-done.7), channel_id=1, source_target_pairs={{0,1},{1,0},{2,3},{3,2},{4,5},{5,4},{6,7},{7,6},{8,9},{9,8},{10,11... | collective-permute-start | bytes 3563528 | tf_op jit(solution)/shard_map/ppermute | solution.py:29
  80.5 1.8 %copy-start.11 = (bf16[480,3712]{1,0:T(8,128)(2,1)}, bf16[480,3712]{1,0:T(8,128)(2,1)S(1)}, u32[]{:S(2)}) copy-start(bf16[480,3712]{1,0:T(8,128)(2,1)S(1)} %get-tuple-element.63) | copy-start | bytes 10690564
  82.3 2.0 %copy-start.12 = (bf16[480,3712]{1,0:T(8,128)(2,1)S(1)}, bf16[480,3712]{1,0:T(8,128)(2,1)}, u32[]{:S(2)}) copy-start(bf16[480,3712]{1,0:T(8,128)(2,1)} %copy-done.11) | copy-start | bytes 10690564
  91.6 6.6 %collective-permute-start.13 = (f32[480]{0:T(512)S(1)}, f32[480]{0:T(512)S(1)}, u32[]{:S(2)}, u32[]{:S(2)}) collective-permute-start(f32[480]{0:T(512)S(1)} %compare_select_fusion.5), channel_id=1, source_target_pairs={{0,1},{1,0},{2,3},{3,2},{4,5},{5,4},{6,7},{7,6},{8,9},{9,8},{10,11... | collective-permute-start | bytes 5768 | tf_op jit(solution)/shard_map/ppermute | solution.py:29
  93.4 5.0 %collective-permute-start.16 = (bf16[160,3712]{1,0:T(8,128)(2,1)S(1)}, bf16[160,3712]{1,0:T(8,128)(2,1)S(1)}, u32[]{:S(2)}, u32[]{:S(2)}) collective-permute-start(bf16[160,3712]{1,0:T(8,128)(2,1)S(1)} %shard_map.130), channel_id=1, source_target_pairs={{0,1},{1,0},{2,3},{3,2},{4,5},{5,4},{6,7},{7,6},{8,9},{9,8},{10,11... | collective-permute-start | bytes 3563528 | tf_op jit(solution)/shard_map/ppermute | solution.py:29
  98.1 6.7 %collective-permute-start.12 = (bf16[480,1792]{1,0:T(8,128)(2,1)S(1)}, bf16[480,1792]{1,0:T(8,128)(2,1)S(1)}, u32[]{:S(2)}, u32[]{:S(2)}) collective-permute-start(bf16[480,1792]{1,0:T(8,128)(2,1)S(1)} %fusion.17), channel_id=1, source_target_pairs={{0,1},{1,0},{2,3},{3,2},{4,5},{5,4},{6,7},{7,6},{8,9},{9,8},{10,11... | collective-permute-start | bytes 5160968 | tf_op jit(solution)/shard_map/ppermute | solution.py:29
  102.1 2.6 %collective-permute-start.18 = (f32[160]{0:T(256)S(1)}, f32[160]{0:T(256)S(1)}, u32[]{:S(2)}, u32[]{:S(2)}) collective-permute-start(f32[160]{0:T(256)S(1)} %compare_select_fusion.4), channel_id=1, source_target_pairs={{0,1},{1,0},{2,3},{3,2},{4,5},{5,4},{6,7},{7,6},{8,9},{9,8},{10,11... | collective-permute-start | bytes 1928 | tf_op jit(solution)/shard_map/ppermute | solution.py:29
  104.6 2.4 %collective-permute-start.17 = (bf16[160,1792]{1,0:T(8,128)(2,1)S(1)}, bf16[160,1792]{1,0:T(8,128)(2,1)S(1)}, u32[]{:S(2)}, u32[]{:S(2)}) collective-permute-start(bf16[160,1792]{1,0:T(8,128)(2,1)S(1)} %fusion.22), channel_id=1, source_target_pairs={{0,1},{1,0},{2,3},{3,2},{4,5},{5,4},{6,7},{7,6},{8,9},{9,8},{10,11... | collective-permute-start | bytes 1720328 | tf_op jit(solution)/shard_map/ppermute | solution.py:29
  108.6 16.2 %collective-permute-start.19 = (bf16[160,1920]{1,0:T(8,128)(2,1)S(1)}, bf16[160,1920]{1,0:T(8,128)(2,1)S(1)}, u32[]{:S(2)}, u32[]{:S(2)}) collective-permute-start(bf16[160,1920]{1,0:T(8,128)(2,1)S(1)} %pad_maximum_fusion.4), channel_id=1, source_target_pairs={{0,2},{1,3},{2,4},{3,5},{4,6},{5,7},{6,0},{7,1},{8,10},{9,11},{10,... | collective-permute-start | bytes 1843208 | tf_op jit(solution)/shard_map/ppermute | solution.py:25
  108.7 16.1 %collective-permute-start.20 = (bf16[160,1920]{1,0:T(8,128)(2,1)S(1)}, bf16[160,1920]{1,0:T(8,128)(2,1)S(1)}, u32[]{:S(2)}, u32[]{:S(2)}) collective-permute-start(bf16[160,1920]{1,0:T(8,128)(2,1)S(1)} %pad_maximum_fusion.5), channel_id=1, source_target_pairs={{0,6},{1,7},{2,0},{3,1},{4,2},{5,3},{6,4},{7,5},{8,14},{9,15},{10,... | collective-permute-start | bytes 1843208 | tf_op jit(solution)/shard_map/ppermute | solution.py:25
  124.9 9.2 %collective-permute-start.21 = (bf16[80,1920]{1,0:T(8,128)(2,1)S(1)}, bf16[80,1920]{1,0:T(8,128)(2,1)S(1)}, u32[]{:S(2)}, u32[]{:S(2)}) collective-permute-start(bf16[80,1920]{1,0:T(8,128)(2,1)S(1)} %get-tuple-element.58), channel_id=1, source_target_pairs={{0,6},{1,7},{2,0},{3,1},{4,2},{5,3},{6,4},{7,5},{8,14},{9,15},{10,... | collective-permute-start | bytes 921608 | tf_op jit(solution)/shard_map/ppermute | solution.py:25
  127.4 8.1 %collective-permute-start.23 = (bf16[80,1920]{1,0:T(8,128)(2,1)S(1)}, bf16[80,1920]{1,0:T(8,128)(2,1)S(1)}, u32[]{:S(2)}, u32[]{:S(2)}) collective-permute-start(bf16[80,1920]{1,0:T(8,128)(2,1)S(1)} %get-tuple-element.59), channel_id=1, source_target_pairs={{0,2},{1,3},{2,4},{3,5},{4,6},{5,7},{6,0},{7,1},{8,10},{9,11},{10,... | collective-permute-start | bytes 921608 | tf_op jit(solution)/shard_map/ppermute | solution.py:25
  135.8 8.7 %collective-permute-start.22 = (bf16[40,1920]{1,0:T(8,128)(2,1)S(1)}, bf16[40,1920]{1,0:T(8,128)(2,1)S(1)}, u32[]{:S(2)}, u32[]{:S(2)}) collective-permute-start(bf16[40,1920]{1,0:T(8,128)(2,1)S(1)} %get-tuple-element.94), channel_id=1, source_target_pairs={{0,24},{8,0},{16,8},{24,16},{32,56},{40,32},{48,40},{56,48},{64,88... | collective-permute-start | bytes 460808 | tf_op jit(solution)/shard_map/ppermute | solution.py:20
  136.5 8.0 %collective-permute-start.24 = (bf16[40,1920]{1,0:T(8,128)(2,1)S(1)}, bf16[40,1920]{1,0:T(8,128)(2,1)S(1)}, u32[]{:S(2)}, u32[]{:S(2)}) collective-permute-start(bf16[40,1920]{1,0:T(8,128)(2,1)S(1)} %get-tuple-element.95), channel_id=1, source_target_pairs={{0,16},{8,24},{16,0},{24,8},{32,48},{40,56},{48,32},{56,40},{64,80... | collective-permute-start | bytes 460808 | tf_op jit(solution)/shard_map/ppermute | solution.py:20
  136.6 7.9 %collective-permute-start.25 = (bf16[40,1920]{1,0:T(8,128)(2,1)S(1)}, bf16[40,1920]{1,0:T(8,128)(2,1)S(1)}, u32[]{:S(2)}, u32[]{:S(2)}) collective-permute-start(bf16[40,1920]{1,0:T(8,128)(2,1)S(1)} %get-tuple-element.96), channel_id=1, source_target_pairs={{0,8},{8,16},{16,24},{24,0},{32,40},{40,48},{48,56},{56,32},{64,72... | collective-permute-start | bytes 460808 | tf_op jit(solution)/shard_map/ppermute | solution.py:20
  144.9 9.7 %collective-permute-start.26 = (bf16[32,1920]{1,0:T(8,128)(2,1)S(1)}, bf16[32,1920]{1,0:T(8,128)(2,1)S(1)}, u32[]{:S(2)}, u32[]{:S(2)}) collective-permute-start(bf16[32,1920]{1,0:T(8,128)(2,1)S(1)} %get-tuple-element.87), channel_id=1, source_target_pairs={{0,96},{8,104},{16,112},{24,120},{32,0},{40,8},{48,16},{56,24},{64... | collective-permute-start | bytes 368648 | tf_op jit(solution)/shard_map/ppermute | solution.py:15
  147.9 6.6 %collective-permute-start.28 = (bf16[32,1920]{1,0:T(8,128)(2,1)S(1)}, bf16[32,1920]{1,0:T(8,128)(2,1)S(1)}, u32[]{:S(2)}, u32[]{:S(2)}) collective-permute-start(bf16[32,1920]{1,0:T(8,128)(2,1)S(1)} %get-tuple-element.88), channel_id=1, source_target_pairs={{0,64},{8,72},{16,80},{24,88},{32,96},{40,104},{48,112},{56,120},{... | collective-permute-start | bytes 368648 | tf_op jit(solution)/shard_map/ppermute | solution.py:15
  148.1 6.5 %collective-permute-start.27 = (bf16[32,1920]{1,0:T(8,128)(2,1)S(1)}, bf16[32,1920]{1,0:T(8,128)(2,1)S(1)}, u32[]{:S(2)}, u32[]{:S(2)}) collective-permute-start(bf16[32,1920]{1,0:T(8,128)(2,1)S(1)} %get-tuple-element.89), channel_id=1, source_target_pairs={{0,32},{8,40},{16,48},{24,56},{32,64},{40,72},{48,80},{56,88},{64,... | collective-permute-start | bytes 368648 | tf_op jit(solution)/shard_map/ppermute | solution.py:15
  154.7 5.8 %collective-permute-start.29 = (bf16[16,1792]{1,0:T(8,128)(2,1)S(1)}, bf16[16,1792]{1,0:T(8,128)(2,1)S(1)}, u32[]{:S(2)}, u32[]{:S(2)}) collective-permute-start(bf16[16,1792]{1,0:T(8,128)(2,1)S(1)} %slice.192), channel_id=1, source_target_pairs={{0,1},{1,0},{2,3},{3,2},{4,5},{5,4},{6,7},{7,6},{8,9},{9,8},{10,11... | collective-permute-start | bytes 172040 | tf_op jit(solution)/shard_map/ppermute | solution.py:29

commit v2 on v1

--- a/solution.py
+++ b/solution.py
@@ -1,3 +1,5 @@
+import functools
+
 import jax
 import jax.numpy as jnp
 from jax import lax
@@ -108,10 +110,22 @@
         copy.wait()
 
 
-def stack_kernel(top, bottom, _, out):
-    side = top.shape[0]
-    out[:side, :] = top[...]
-    out[side:, :] = bottom[...]
+def stack_kernel(count, *refs):
+    start = 0
+    for ref in refs[:count]:
+        refs[-1][pl.ds(start, ref.shape[0]), :] = ref[...]
+        start += ref.shape[0]
+
+
+def stack(parts, *done):
+    shape = (sum(part.shape[0] for part in parts), parts[0].shape[1])
+    return pl.pallas_call(
+        functools.partial(stack_kernel, len(parts)),
+        out_shape=jax.ShapeDtypeStruct(shape, BF),
+        in_specs=vmem(len(parts) + len(done)),
+        out_specs=vmem(1)[0],
+        compiler_params=limit(6),
+    )(*parts, *done)
 
 
 def per_device(
@@ -136,7 +150,6 @@
         out_shape=[jax.ShapeDtypeStruct((tok, width + TAIL), BF)] * 2,
         in_specs=[pl.BlockSpec(memory_space=pltpu.SMEM)] + [pl.BlockSpec()] * 6,
         out_specs=vmem(2),
-        compiler_params=limit(4),
     )(
         core_arg,
         tokens,
@@ -185,8 +198,12 @@
         compiler_params=limit(14),
     )(core_arg, gate_w[0], up_w[0], down_w[0], raw_send)
 
-    mine = jnp.concatenate(exchange_z(parts, 1), axis=0)
-    below, above = along_y(mine, 1), along_y(mine, -1)
+    parts = exchange_z(parts, 1)
+    first_below, first_above = along_y(parts[0], 1), along_y(parts[0], -1)
+    rest = stack(parts[1:], first_below, first_above)
+    mine = jnp.concatenate([parts[0], rest], axis=0)
+    below = jnp.concatenate([first_below, along_y(rest, 1)], axis=0)
+    above = jnp.concatenate([first_above, along_y(rest, -1)], axis=0)
     far_parts = along_y(below[:side], 1), along_y(above[side:], -1)
     near = [mine, below, above]
     tail_lane = jnp.arange(TAIL, dtype=jnp.int32)[None, :]
@@ -225,31 +242,22 @@
     near_state, near_full = row_gradients(
         jnp.concatenate(near, axis=0), jnp.concatenate([across(p) for p in near], axis=0)
     )
-    far = pl.pallas_call(
-        stack_kernel,
-        out_shape=jax.ShapeDtypeStruct((2 * side, rows.shape[1]), BF),
-        in_specs=vmem(3),
-        out_specs=vmem(1)[0],
-        compiler_params=limit(4),
-    )(*far_parts, near_state[2])
+    far = stack(far_parts, near_state[2])
     far_state, far_full = row_gradients(far, across(far))
 
     near_full, far_full = lax.optimization_barrier((near_full, far_full))
-    own_top, own_bottom, below_top, below_bottom, above_top, above_bottom = jnp.split(
-        near_full, 6, axis=0
-    )
-    from_above = along_y(jnp.concatenate([far_full[:side], below_bottom], axis=0), -1)
-    from_below = along_y(jnp.concatenate([far_full[side:], above_top], axis=0), 1)
-    early_top, early_bottom = from_below[side:], from_above[side:]
-    late_top = along_y(below_top + from_above[:side], -1)
-    late_bottom = along_y(above_bottom + from_below[:side], 1)
+    own_rows, below_rows, above_rows = jnp.split(near_full, 3, axis=0)
+    back_parts = [
+        own_rows,
+        along_y(below_rows, -1),
+        along_y(above_rows, 1),
+        along_y(far_full, 2),
+    ]
 
     def add(*parts):
         return sum(p.astype(F32) for p in parts).astype(BF)
 
-    top_rows = add(own_top, early_top, late_top)
-    bottom_rows = add(own_bottom, early_bottom, late_bottom)
-    back = [top_rows[:slots], top_rows[slots:], bottom_rows[:slots], bottom_rows[slots:]]
+    back = jnp.split(add(*back_parts), 4, axis=0)
     back = jnp.concatenate(exchange_z(back, -1), axis=0)
     parts = jnp.split(tn(select, back).astype(BF), 4, axis=0)
     parts = [parts[0], along_x(parts[1], -1), along_x(parts[2], 1), along_x(parts[3], 2)]

time: 162 us -> 162 us (level)
  local copies, waits for them, and re-layouts: 17.7 us -> 11.8 us
  waiting for transfers between devices: 58 us -> 63.1 us
  starting transfers between devices: 39.1 us -> 36.8 us
  matrix products: 37.7 us -> 39.9 us
  Pallas kernels: 1.78 us -> 3.5 us
    unnamed x39 -> x25, local copies, waits for them, and re-layouts: 16.4 us -> 10.4 us
    ppermute x8 -> x9, waiting for transfers between devices: 41.1 us -> 44.1 us  [along_y(): return lax.ppermute(value, 'local', pairs)]
    dot_general x19, matrix products: 37.7 us -> 39.9 us  [dot(): lax.dot_general(left, right, ((dims[0], dims[1]), ((), ())), preferred_el...]
    ppermute x8 -> x9, starting transfers between devices: 11.6 us -> 9.8 us  [along_y(): return lax.ppermute(value, 'local', pairs)]
    pallas_call x1, Pallas kernels: 0.2 us -> 1.86 us  [per_device(): pl.pallas_call(start_kernel, out_shape=[jax.ShapeDtypeStruct((tok, width...]
  transfers between devices with their start and end apart: 30 -> 31, of which waited for: 9 -> 14; matrix products, arithmetic and copies ran while one was open for 27% -> 29% of each run, Pallas kernels for 1% -> 1%
where the time goes in v2:
time: 162 us
  waiting for transfers between devices  63.1 us (39%)
  matrix products  39.9 us (25%)
  starting transfers between devices  36.8 us (23%)
  local copies, waits for them, and re-layouts  11.8 us (7%)
  other arithmetic  5.75 us (4%)
  Pallas kernels  3.5 us (2%)
    ppermute x9, waiting for transfers between devices, along_y(): return lax.ppermute(value, 'local', pairs)  44.1 us
    dot_general x19, matrix products, dot(): lax.dot_general(left, right, ((dims[0], dims[1]), ((), ())), preferred_el...  39.9 us
    ppermute x10, starting transfers between devices, across(): return lax.ppermute(value, 'local', [(i, i ^ 1) for i in range(8)])  10.8 us
    unnamed x25, local copies, waits for them, and re-layouts  10.4 us
    ppermute x9, starting transfers between devices, along_y(): return lax.ppermute(value, 'local', pairs)  9.8 us
    ppermute x6, waiting for transfers between devices, along_x(): return lax.ppermute(value, 'node', pairs)  9.1 us
    ppermute x6, starting transfers between devices, along_x(): return lax.ppermute(value, 'node', pairs)  8.93 us
    ppermute x6, waiting for transfers between devices, along_z(): return lax.ppermute(value, 'node', pairs)  8.3 us
  transfers between devices with their start and end apart: 31, of which 14 were waited for; matrix products, arithmetic and copies ran while one was open for 29% of the time, Pallas kernels for 1%

profile of v2, /device:TPU:1, one launch (start us, length us, event | category | flops | bytes accessed | tf_op | source)
XLA Modules:
  0.0 162.0 jit_solution(8101947325251501260)
XLA Ops:
  0.6 1.9 %shard_map.128 = (bf16[16,3712]{1,0:T(8,128)(2,1)}, bf16[16,3712]{1,0:T(8,128)(2,1)}) custom-call(s32[1]{0:T(128)} %bitcast.core, bf16[16,3584]{1,0:T(8,128)(2,1)} %tok.1, bf16[16,3584]{1,0:T(8,128)(2,1)} %cot.1, s32[4,16]{1,0:T(4,128)} %bitcast.38, s32[1,16]{1,0:T(1,128)} %homes.1, s32[4,16]{1,0:T(4,128)} %bitcast.40, bf16[8,16]{1,0:T(8,128)(2,1)} %bitcast.41), custom_call_target="tpu_custom_call" | custom-call | tf_op jit(solution)/shard_map/pallas_call | solution.py:148
  2.5 1.4 collective-permute-start
  3.9 0.7 broadcast_multiply_fusion.2
  4.6 0.9 constant_dynamic-update-slice_fusion.1
  5.6 0.9 select_reduce_fusion.3
  6.5 1.4 collective-permute-start.1
  8.0 0.7 fusion.75
  8.7 2.5 %collective-permute-start.3 = (bf16[32,3712]{1,0:T(8,128)(2,1)S(1)}, bf16[32,3712]{1,0:T(8,128)(2,1)S(1)}, u32[]{:S(2)}, u32[]{:S(2)}) collective-permute-start(bf16[32,3712]{1,0:T(8,128)(2,1)S(1)} %get-tuple-element.101), channel_id=1, source_target_pairs={{0,64},{8,72},{16,80},{24,88},{32,96},{40,104},{48,112},{56,120},{... | collective-permute-start | bytes 712712 | tf_op jit(solution)/shard_map/ppermute | solution.py:17
  11.2 1.2 collective-permute-start.2
  12.3 2.9 %collective-permute-done.1 = bf16[32,3712]{1,0:T(8,128)(2,1)S(1)} collective-permute-done((bf16[32,3712]{1,0:T(8,128)(2,1)S(1)}, bf16[32,3712]{1,0:T(8,128)(2,1)S(1)}, u32[]{:S(2)}, u32[]{:S(2)}) %collective-permute-start.1) | collective-permute-done | bytes 237600 | tf_op jit(solution)/shard_map/ppermute | solution.py:17
  15.3 6.2 %collective-permute-done.2 = bf16[32,3712]{1,0:T(8,128)(2,1)S(1)} collective-permute-done((bf16[32,3712]{1,0:T(8,128)(2,1)S(1)}, bf16[32,3712]{1,0:T(8,128)(2,1)S(1)}, u32[]{:S(2)}, u32[]{:S(2)}) %collective-permute-start.2) | collective-permute-done | bytes 237600 | tf_op jit(solution)/shard_map/ppermute | solution.py:17
  22.1 0.5 convolution_convert_fusion.3
  22.5 0.9 constant_dynamic-update-slice_fusion.24
  23.5 2.8 %collective-permute-start.8 = (bf16[40,3712]{1,0:T(8,128)(2,1)S(1)}, bf16[40,3712]{1,0:T(8,128)(2,1)S(1)}, u32[]{:S(2)}, u32[]{:S(2)}) collective-permute-start(bf16[40,3712]{1,0:T(8,128)(2,1)S(1)} %get-tuple-element.63), channel_id=1, source_target_pairs={{0,6},{1,7},{2,0},{3,1},{4,2},{5,3},{6,4},{7,5},{8,14},{9,15},{10,... | collective-permute-start | bytes 890888 | tf_op jit(solution)/shard_map/ppermute | solution.py:27
  26.3 3.8 %collective-permute-start.6 = (bf16[40,3712]{1,0:T(8,128)(2,1)S(1)}, bf16[40,3712]{1,0:T(8,128)(2,1)S(1)}, u32[]{:S(2)}, u32[]{:S(2)}) collective-permute-start(bf16[40,3712]{1,0:T(8,128)(2,1)S(1)} %get-tuple-element.60), channel_id=1, source_target_pairs={{0,24},{8,0},{16,8},{24,16},{32,56},{40,32},{48,40},{56,48},{64,88... | collective-permute-start | bytes 890888 | tf_op jit(solution)/shard_map/ppermute | solution.py:22
  30.0 0.7 collective-permute-start.4
  30.8 2.0 %copy-done = bf16[1,3584,512]{2,1,0:T(8,128)(2,1)S(1)} copy-done((bf16[1,3584,512]{2,1,0:T(8,128)(2,1)S(1)}, bf16[1,3584,512]{2,1,0:T(8,128)(2,1)}, u32[]{:S(2)}) %copy-start) | copy-done | bytes 3670040
  32.9 2.0 %copy-done.1 = bf16[1,3584,512]{2,1,0:T(8,128)(2,1)S(1)} copy-done((bf16[1,3584,512]{2,1,0:T(8,128)(2,1)S(1)}, bf16[1,3584,512]{2,1,0:T(8,128)(2,1)}, u32[]{:S(2)}) %copy-start.1) | copy-done | bytes 3670040
  34.9 2.0 %copy-done.2 = bf16[1,512,3584]{2,1,0:T(8,128)(2,1)S(1)} copy-done((bf16[1,512,3584]{2,1,0:T(8,128)(2,1)S(1)}, bf16[1,512,3584]{2,1,0:T(8,128)(2,1)}, u32[]{:S(2)}) %copy-start.2) | copy-done | bytes 3670040
  36.9 1.5 shard_map.130
  38.5 2.7 %collective-permute-done.6.refs_2_ = bf16[40,3712]{1,0:T(8,128)(2,1)S(1)} collective-permute-done((bf16[40,3712]{1,0:T(8,128)(2,1)S(1)}, bf16[40,3712]{1,0:T(8,128)(2,1)S(1)}, u32[]{:S(2)}, u32[]{:S(2)}) %collective-permute-start.6) | collective-permute-done | bytes 296992 | tf_op jit(solution)/shard_map/ppermute | solution.py:22
  41.2 5.0 %collective-permute-done.4.refs_0_ = bf16[40,3712]{1,0:T(8,128)(2,1)S(1)} collective-permute-done((bf16[40,3712]{1,0:T(8,128)(2,1)S(1)}, bf16[40,3712]{1,0:T(8,128)(2,1)S(1)}, u32[]{:S(2)}, u32[]{:S(2)}) %collective-permute-start.4) | collective-permute-done | bytes 296992 | tf_op jit(solution)/shard_map/ppermute | solution.py:22
  46.4 2.7 %collective-permute-start.10 = (bf16[120,3712]{1,0:T(8,128)(2,1)S(1)}, bf16[120,3712]{1,0:T(8,128)(2,1)S(1)}, u32[]{:S(2)}, u32[]{:S(2)}) collective-permute-start(bf16[120,3712]{1,0:T(8,128)(2,1)S(1)} %shard_map.129), channel_id=1, source_target_pairs={{0,6},{1,7},{2,0},{3,1},{4,2},{5,3},{6,4},{7,5},{8,14},{9,15},{10,... | collective-permute-start | bytes 2672648 | tf_op jit(solution)/shard_map/ppermute | solution.py:27
  49.1 1.1 collective-permute-start.11
  50.6 19.9 %collective-permute-done.9 = bf16[120,3712]{1,0:T(8,128)(2,1)S(1)} collective-permute-done((bf16[120,3712]{1,0:T(8,128)(2,1)S(1)}, bf16[120,3712]{1,0:T(8,128)(2,1)S(1)}, u32[]{:S(2)}, u32[]{:S(2)}) %collective-permute-start.9) | collective-permute-done | bytes 890912 | tf_op jit(solution)/shard_map/ppermute | solution.py:27
  70.5 0.3 constant_dynamic-update-slice_fusion.21
  70.9 2.1 %collective-permute-start.12 = (bf16[160,3712]{1,0:T(8,128)(2,1)S(1)}, bf16[160,3712]{1,0:T(8,128)(2,1)S(1)}, u32[]{:S(2)}, u32[]{:S(2)}) collective-permute-start(bf16[160,3712]{1,0:T(8,128)(2,1)S(1)} %get-tuple-element.76), channel_id=1, source_target_pairs={{0,1},{1,0},{2,3},{3,2},{4,5},{5,4},{6,7},{7,6},{8,9},{9,8},{10,11... | collective-permute-start | bytes 3563528 | tf_op jit(solution)/shard_map/ppermute | solution.py:31
  73.2 1.5 collective-permute-start.16
  74.7 0.8 collective-permute-start.13
  76.5 1.6 collective-permute-done.13
  78.3 1.1 fusion.29
  79.4 2.3 %fusion.25 = f32[480,1024]{1,0:T(8,128)S(1)} fusion(bf16[1920,1024]{1,0:T(8,128)(2,1)S(1)} %get-tuple-element.26, bf16[480,3712]{1,0:T(8,128)(2,1)S(1)} %get-tuple-element.65), kind=kOutput, calls=%fused_computation.27 | convolution fusion | flops 1887436800 | bytes 7741440 | tf_op jit(solution)/shard_map/dot_general | solution.py:35
  81.7 2.3 %fusion.33 = f32[480,1024]{1,0:T(8,128)S(1)} fusion(f32[480,1024]{1,0:T(8,128)S(1)} %fusion.25, bf16[1920,1024]{1,0:T(8,128)(2,1)S(1)} %get-tuple-element.25, bf16[480,3712]{1,0:T(8,128)(2,1)S(1)} %get-tuple-element.74), kind=kOutput, calls=%fused_computation.36 | convolution fusion | flops 1887928320 | bytes 9707520 | tf_op jit(solution)/shard_map/dot_general | solution.py:35
  84.0 0.6 broadcast_multiply_fusion
  84.5 1.3 multiply_convert_fusion.1
  85.9 0.5 collective-permute-start.15
  86.5 1.7 %collective-permute-done.17.refs_1_ = bf16[80,3712]{1,0:T(8,128)(2,1)S(1)} collective-permute-done((bf16[80,3712]{1,0:T(8,128)(2,1)S(1)}, bf16[80,3712]{1,0:T(8,128)(2,1)S(1)}, u32[]{:S(2)}, u32[]{:S(2)}) %collective-permute-start.17) | collective-permute-done | bytes 593952 | tf_op jit(solution)/shard_map/ppermute | solution.py:27
  88.2 1.3 collective-permute-done.16.refs_0_
  89.5 0.9 collective-permute-start.18
  90.9 3.2 %fusion.17 = bf16[480,1792]{1,0:T(8,128)(2,1)} fusion(bf16[1920,1024]{1,0:T(8,128)(2,1)S(1)} %get-tuple-element.26, bf16[480,512]{1,0:T(8,128)(2,1)S(1)} %get-tuple-element.72, bf16[480,512]{1,0:T(8,128)(2,1)S(1)} %get-tuple-element.70), kind=kOutput, calls=%fused_computation.24 | convolution fusion | flops 1764433920 | bytes 6373376 | tf_op jit(solution)/shard_map/dot_general | solution.py:35
  94.5 0.8 fusion.47
  95.4 0.9 convolution_add_fusion
  96.4 0.7 fusion.57
  97.2 0.9 multiply_convert_fusion.5
  98.1 0.8 collective-permute-start.20
  99.0 1.3 fusion.22
  101.1 3.4 %add_convert_fusion = bf16[480,1792]{1,0:T(8,128)(2,1)S(1)} fusion(bf16[480,1792]{1,0:T(8,128)(2,1)} %collective-permute-done.14, bf16[1920,1024]{1,0:T(8,128)(2,1)S(1)} %get-tuple-element.25, bf16[480,512]{1,0:T(8,128)(2,1)S(1)} %get-tuple-element.72, bf16[480,512]{1,0:T(8,128)(2,1)S(1)} %get-tuple-element.70), kind=kOutput, calls=%fused_computation.15 | convolution fusion | flops 1766154240 | bytes 8093696 | tf_op jit(solution)/shard_map/dot_general | solution.py:35
  104.7 1.4 add_convert_fusion.2
  106.1 0.6 collective-permute-start.23
  106.8 2.1 %collective-permute-start.21 = (bf16[160,1920]{1,0:T(8,128)(2,1)S(1)}, bf16[160,1920]{1,0:T(8,128)(2,1)S(1)}, u32[]{:S(2)}, u32[]{:S(2)}) collective-permute-start(bf16[160,1920]{1,0:T(8,128)(2,1)S(1)} %get-tuple-element.56), channel_id=1, source_target_pairs={{0,6},{1,7},{2,0},{3,1},{4,2},{5,3},{6,4},{7,5},{8,14},{9,15},{10,... | collective-permute-start | bytes 1843208 | tf_op jit(solution)/shard_map/ppermute | solution.py:27
  109.0 6.6 %fusion.1 = bf16[1,3584,512]{2,1,0:T(8,128)(2,1)} fusion(bf16[640,1792]{1,0:T(8,128)(2,1)S(1)} %get-tuple-element.51, bf16[640,1792]{1,0:T(8,128)(2,1)S(1)} %get-tuple-element.49, pred[]{:T(512)S(6)} %eq.114, bf16[640,1024]{1,0:T(8,128)(2,1)S(1)} %maximum_maximum_fusion), kind=kOutput, calls=%fused_computation.4 | convolution fusion | flops 2371289088 | bytes 8912897 | tf_op jit(solution)/shard_map/dot_general | solution.py:35
  115.5 7.2 %collective-permute-done.23 = bf16[160,1920]{1,0:T(8,128)(2,1)S(1)} collective-permute-done((bf16[160,1920]{1,0:T(8,128)(2,1)S(1)}, bf16[160,1920]{1,0:T(8,128)(2,1)S(1)}, u32[]{:S(2)}, u32[]{:S(2)}) %collective-permute-start.23) | collective-permute-done | bytes 614432 | tf_op jit(solution)/shard_map/ppermute | solution.py:27
  122.7 10.7 %collective-permute-done.21 = bf16[160,1920]{1,0:T(8,128)(2,1)S(1)} collective-permute-done((bf16[160,1920]{1,0:T(8,128)(2,1)S(1)}, bf16[160,1920]{1,0:T(8,128)(2,1)S(1)}, u32[]{:S(2)}, u32[]{:S(2)}) %collective-permute-start.21) | collective-permute-done | bytes 614432 | tf_op jit(solution)/shard_map/ppermute | solution.py:27
  133.4 3.2 %collective-permute-done.22 = bf16[160,1920]{1,0:T(8,128)(2,1)S(1)} collective-permute-done((bf16[160,1920]{1,0:T(8,128)(2,1)S(1)}, bf16[160,1920]{1,0:T(8,128)(2,1)S(1)}, u32[]{:S(2)}, u32[]{:S(2)}) %collective-permute-start.22) | collective-permute-done | bytes 614432 | tf_op jit(solution)/shard_map/ppermute | solution.py:27
  137.1 0.7 collective-permute-start.25
  137.9 2.0 %collective-permute-start.24 = (bf16[40,1920]{1,0:T(8,128)(2,1)S(1)}, bf16[40,1920]{1,0:T(8,128)(2,1)S(1)}, u32[]{:S(2)}, u32[]{:S(2)}) collective-permute-start(bf16[40,1920]{1,0:T(8,128)(2,1)S(1)} %get-tuple-element.87), channel_id=1, source_target_pairs={{0,24},{8,0},{16,8},{24,16},{32,56},{40,32},{48,40},{56,48},{64,88... | collective-permute-start | bytes 460808 | tf_op jit(solution)/shard_map/ppermute | solution.py:22
  139.8 6.6 %fusion = bf16[1,3584,512]{2,1,0:T(8,128)(2,1)} fusion(bf16[640,1792]{1,0:T(8,128)(2,1)S(1)} %get-tuple-element.51, bf16[640,1792]{1,0:T(8,128)(2,1)S(1)} %get-tuple-element.49, pred[]{:T(512)S(6)} %eq.114, bf16[640,1024]{1,0:T(8,128)(2,1)S(1)} %maximum_maximum_fusion), kind=kOutput, calls=%fused_computation.3 | convolution fusion | flops 2371289088 | bytes 8912897 | tf_op jit(solution)/shard_map/dot_general | solution.py:35
  146.4 0.4 collective-permute-done.26
  147.4 3.0 %collective-permute-start.27 = (bf16[32,1920]{1,0:T(8,128)(2,1)S(1)}, bf16[32,1920]{1,0:T(8,128)(2,1)S(1)}, u32[]{:S(2)}, u32[]{:S(2)}) collective-permute-start(bf16[32,1920]{1,0:T(8,128)(2,1)S(1)} %get-tuple-element.88), channel_id=1, source_target_pairs={{0,96},{8,104},{16,112},{24,120},{32,0},{40,8},{48,16},{56,24},{64... | collective-permute-start | bytes 368648 | tf_op jit(solution)/shard_map/ppermute | solution.py:17
  150.6 0.7 collective-permute-start.28
  151.4 5.9 %fusion.2 = bf16[1,512,3584]{2,1,0:T(8,128)(2,1)} fusion(bf16[640,1792]{1,0:T(8,128)(2,1)S(1)} %get-tuple-element.50, bf16[640,1792]{1,0:T(8,128)(2,1)S(1)} %get-tuple-element.48, pred[]{:T(512)S(6)} %eq.114, bf16[160,512]{1,0:T(8,128)(2,1)S(1)} %get-tuple-element.36, bf16[480,512]{1,0:T(8,128)(2,1)S(1)} %get-tuple-element.35), kind=kOutput, calls=%fused_computation.5 | convolution fusion | flops 2372599808 | bytes 8912897 | tf_op jit(solution)/shard_map/dot_general | solution.py:35
  157.4 3.0 %collective-permute-start.30 = (bf16[16,1792]{1,0:T(8,128)(2,1)S(1)}, bf16[16,1792]{1,0:T(8,128)(2,1)S(1)}, u32[]{:S(2)}, u32[]{:S(2)}) collective-permute-start(bf16[16,1792]{1,0:T(8,128)(2,1)S(1)} %slice.144), channel_id=1, source_target_pairs={{0,1},{1,0},{2,3},{3,2},{4,5},{5,4},{6,7},{7,6},{8,9},{9,8},{10,11... | collective-permute-start | bytes 172040 | tf_op jit(solution)/shard_map/ppermute | solution.py:31
  160.6 0.7 copy.19
  161.3 0.7 pad_maximum_fusion.10
  (97 shorter events, 6.8 us)
Async XLA Ops:
  2.5 4.0 %collective-permute-start = (bf16[16,3712]{1,0:T(8,128)(2,1)}, bf16[16,3712]{1,0:T(8,128)(2,1)S(1)}, u32[]{:S(2)}, u32[]{:S(2)}) collective-permute-start(bf16[16,3712]{1,0:T(8,128)(2,1)} %get-tuple-element.22._), channel_id=1, source_target_pairs={{0,1},{1,0},{2,3},{3,2},{4,5},{5,4},{6,7},{7,6},{8,9},{9,8},{10,11... | collective-permute-start | bytes 356360 | tf_op jit(solution)/shard_map/ppermute | solution.py:31
  6.5 24.3 %copy-start.3 = (bf16[16,3712]{1,0:T(8,128)(2,1)S(1)}, bf16[16,3712]{1,0:T(8,128)(2,1)}, u32[]{:S(2)}) copy-start(bf16[16,3712]{1,0:T(8,128)(2,1)} %get-tuple-element.22._) | copy-start | bytes 356356
  6.5 8.7 %collective-permute-start.1 = (bf16[32,3712]{1,0:T(8,128)(2,1)S(1)}, bf16[32,3712]{1,0:T(8,128)(2,1)S(1)}, u32[]{:S(2)}, u32[]{:S(2)}) collective-permute-start(bf16[32,3712]{1,0:T(8,128)(2,1)S(1)} %get-tuple-element.101), channel_id=1, source_target_pairs={{0,32},{8,40},{16,48},{24,56},{32,64},{40,72},{48,80},{56,88},{64,... | collective-permute-start | bytes 712712 | tf_op jit(solution)/shard_map/ppermute | solution.py:17
  8.7 12.7 %collective-permute-start.3 = (bf16[32,3712]{1,0:T(8,128)(2,1)S(1)}, bf16[32,3712]{1,0:T(8,128)(2,1)S(1)}, u32[]{:S(2)}, u32[]{:S(2)}) collective-permute-start(bf16[32,3712]{1,0:T(8,128)(2,1)S(1)} %get-tuple-element.101), channel_id=1, source_target_pairs={{0,64},{8,72},{16,80},{24,88},{32,96},{40,104},{48,112},{56,120},{... | collective-permute-start | bytes 712712 | tf_op jit(solution)/shard_map/ppermute | solution.py:17
  11.2 10.3 %collective-permute-start.2 = (bf16[32,3712]{1,0:T(8,128)(2,1)S(1)}, bf16[32,3712]{1,0:T(8,128)(2,1)S(1)}, u32[]{:S(2)}, u32[]{:S(2)}) collective-permute-start(bf16[32,3712]{1,0:T(8,128)(2,1)S(1)} %get-tuple-element.101), channel_id=1, source_target_pairs={{0,96},{8,104},{16,112},{24,120},{32,0},{40,8},{48,16},{56,24},{64... | collective-permute-start | bytes 712712 | tf_op jit(solution)/shard_map/ppermute | solution.py:17
  23.5 22.8 %collective-permute-start.8 = (bf16[40,3712]{1,0:T(8,128)(2,1)S(1)}, bf16[40,3712]{1,0:T(8,128)(2,1)S(1)}, u32[]{:S(2)}, u32[]{:S(2)}) collective-permute-start(bf16[40,3712]{1,0:T(8,128)(2,1)S(1)} %get-tuple-element.63), channel_id=1, source_target_pairs={{0,6},{1,7},{2,0},{3,1},{4,2},{5,3},{6,4},{7,5},{8,14},{9,15},{10,... | collective-permute-start | bytes 890888 | tf_op jit(solution)/shard_map/ppermute | solution.py:27
  26.3 20.0 %collective-permute-start.7 = (bf16[40,3712]{1,0:T(8,128)(2,1)S(1)}, bf16[40,3712]{1,0:T(8,128)(2,1)S(1)}, u32[]{:S(2)}, u32[]{:S(2)}) collective-permute-start(bf16[40,3712]{1,0:T(8,128)(2,1)S(1)} %get-tuple-element.63), channel_id=1, source_target_pairs={{0,2},{1,3},{2,4},{3,5},{4,6},{5,7},{6,0},{7,1},{8,10},{9,11},{10,... | collective-permute-start | bytes 890888 | tf_op jit(solution)/shard_map/ppermute | solution.py:27
  26.3 14.9 %collective-permute-start.6 = (bf16[40,3712]{1,0:T(8,128)(2,1)S(1)}, bf16[40,3712]{1,0:T(8,128)(2,1)S(1)}, u32[]{:S(2)}, u32[]{:S(2)}) collective-permute-start(bf16[40,3712]{1,0:T(8,128)(2,1)S(1)} %get-tuple-element.60), channel_id=1, source_target_pairs={{0,24},{8,0},{16,8},{24,16},{32,56},{40,32},{48,40},{56,48},{64,88... | collective-permute-start | bytes 890888 | tf_op jit(solution)/shard_map/ppermute | solution.py:22
  30.0 11.2 %collective-permute-start.5 = (bf16[40,3712]{1,0:T(8,128)(2,1)S(1)}, bf16[40,3712]{1,0:T(8,128)(2,1)S(1)}, u32[]{:S(2)}, u32[]{:S(2)}) collective-permute-start(bf16[40,3712]{1,0:T(8,128)(2,1)S(1)} %get-tuple-element.61), channel_id=1, source_target_pairs={{0,16},{8,24},{16,0},{24,8},{32,48},{40,56},{48,32},{56,40},{64,80... | collective-permute-start | bytes 890888 | tf_op jit(solution)/shard_map/ppermute | solution.py:22
  30.0 16.2 %collective-permute-start.4 = (bf16[40,3712]{1,0:T(8,128)(2,1)S(1)}, bf16[40,3712]{1,0:T(8,128)(2,1)S(1)}, u32[]{:S(2)}, u32[]{:S(2)}) collective-permute-start(bf16[40,3712]{1,0:T(8,128)(2,1)S(1)} %get-tuple-element.62), channel_id=1, source_target_pairs={{0,8},{8,16},{16,24},{24,0},{32,40},{40,48},{48,56},{56,32},{64,72... | collective-permute-start | bytes 890888 | tf_op jit(solution)/shard_map/ppermute | solution.py:22
  30.8 2.0 %copy-start = (bf16[1,3584,512]{2,1,0:T(8,128)(2,1)S(1)}, bf16[1,3584,512]{2,1,0:T(8,128)(2,1)}, u32[]{:S(2)}) copy-start(bf16[1,3584,512]{2,1,0:T(8,128)(2,1)} %param.15) | copy-start | bytes 11010052
  32.9 2.0 %copy-start.1 = (bf16[1,3584,512]{2,1,0:T(8,128)(2,1)S(1)}, bf16[1,3584,512]{2,1,0:T(8,128)(2,1)}, u32[]{:S(2)}) copy-start(bf16[1,3584,512]{2,1,0:T(8,128)(2,1)} %param.16) | copy-start | bytes 11010052
  34.9 2.0 %copy-start.2 = (bf16[1,512,3584]{2,1,0:T(8,128)(2,1)S(1)}, bf16[1,512,3584]{2,1,0:T(8,128)(2,1)}, u32[]{:S(2)}) copy-start(bf16[1,512,3584]{2,1,0:T(8,128)(2,1)} %param.17) | copy-start | bytes 11010052
  36.9 13.3 %copy-start.5 = (bf16[480,3712]{1,0:T(8,128)(2,1)S(1)}, bf16[480,3712]{1,0:T(8,128)(2,1)}, u32[]{:S(2)}) copy-start(bf16[480,3712]{1,0:T(8,128)(2,1)} %get-tuple-element.59) | copy-start | bytes 10690564
  38.5 11.8 %copy-start.4 = (bf16[640,3712]{1,0:T(8,128)(2,1)S(1)}, bf16[640,3712]{1,0:T(8,128)(2,1)}, u32[]{:S(2)}) copy-start(bf16[640,3712]{1,0:T(8,128)(2,1)} %get-tuple-element.58) | copy-start | bytes 14254084
  46.4 26.6 %collective-permute-start.10 = (bf16[120,3712]{1,0:T(8,128)(2,1)S(1)}, bf16[120,3712]{1,0:T(8,128)(2,1)S(1)}, u32[]{:S(2)}, u32[]{:S(2)}) collective-permute-start(bf16[120,3712]{1,0:T(8,128)(2,1)S(1)} %shard_map.129), channel_id=1, source_target_pairs={{0,6},{1,7},{2,0},{3,1},{4,2},{5,3},{6,4},{7,5},{8,14},{9,15},{10,... | collective-permute-start | bytes 2672648 | tf_op jit(solution)/shard_map/ppermute | solution.py:27
  49.1 21.4 %collective-permute-start.9 = (bf16[120,3712]{1,0:T(8,128)(2,1)S(1)}, bf16[120,3712]{1,0:T(8,128)(2,1)S(1)}, u32[]{:S(2)}, u32[]{:S(2)}) collective-permute-start(bf16[120,3712]{1,0:T(8,128)(2,1)S(1)} %shard_map.129), channel_id=1, source_target_pairs={{0,2},{1,3},{2,4},{3,5},{4,6},{5,7},{6,0},{7,1},{8,10},{9,11},{10,... | collective-permute-start | bytes 2672648 | tf_op jit(solution)/shard_map/ppermute | solution.py:27
  49.1 26.8 %collective-permute-start.11 = (bf16[160,3712]{1,0:T(8,128)(2,1)S(1)}, bf16[160,3712]{1,0:T(8,128)(2,1)S(1)}, u32[]{:S(2)}, u32[]{:S(2)}) collective-permute-start(bf16[160,3712]{1,0:T(8,128)(2,1)S(1)} %pad_maximum_fusion.1), channel_id=1, source_target_pairs={{0,1},{1,0},{2,3},{3,2},{4,5},{5,4},{6,7},{7,6},{8,9},{9,8},{10,11... | collective-permute-start | bytes 3563528 | tf_op jit(solution)/shard_map/ppermute | solution.py:31
  70.9 5.3 %collective-permute-start.12 = (bf16[160,3712]{1,0:T(8,128)(2,1)S(1)}, bf16[160,3712]{1,0:T(8,128)(2,1)S(1)}, u32[]{:S(2)}, u32[]{:S(2)}) collective-permute-start(bf16[160,3712]{1,0:T(8,128)(2,1)S(1)} %get-tuple-element.76), channel_id=1, source_target_pairs={{0,1},{1,0},{2,3},{3,2},{4,5},{5,4},{6,7},{7,6},{8,9},{9,8},{10,11... | collective-permute-start | bytes 3563528 | tf_op jit(solution)/shard_map/ppermute | solution.py:31
  73.1 15.1 %collective-permute-start.17 = (bf16[80,3712]{1,0:T(8,128)(2,1)S(1)}, bf16[80,3712]{1,0:T(8,128)(2,1)S(1)}, u32[]{:S(2)}, u32[]{:S(2)}) collective-permute-start(bf16[80,3712]{1,0:T(8,128)(2,1)S(1)} %slice.135), channel_id=1, source_target_pairs={{0,6},{1,7},{2,0},{3,1},{4,2},{5,3},{6,4},{7,5},{8,14},{9,15},{10,... | collective-permute-start | bytes 1781768 | tf_op jit(solution)/shard_map/ppermute | solution.py:27
  73.2 16.3 %collective-permute-start.16 = (bf16[80,3712]{1,0:T(8,128)(2,1)S(1)}, bf16[80,3712]{1,0:T(8,128)(2,1)S(1)}, u32[]{:S(2)}, u32[]{:S(2)}) collective-permute-start(bf16[80,3712]{1,0:T(8,128)(2,1)S(1)} %slice.134), channel_id=1, source_target_pairs={{0,2},{1,3},{2,4},{3,5},{4,6},{5,7},{6,0},{7,1},{8,10},{9,11},{10,... | collective-permute-start | bytes 1781768 | tf_op jit(solution)/shard_map/ppermute | solution.py:27
  74.7 3.3 %collective-permute-start.13 = (bf16[160,3712]{1,0:T(8,128)(2,1)S(1)}, bf16[160,3712]{1,0:T(8,128)(2,1)S(1)}, u32[]{:S(2)}, u32[]{:S(2)}) collective-permute-start(bf16[160,3712]{1,0:T(8,128)(2,1)S(1)} %pad_maximum_fusion.2), channel_id=1, source_target_pairs={{0,1},{1,0},{2,3},{3,2},{4,5},{5,4},{6,7},{7,6},{8,9},{9,8},{10,11... | collective-permute-start | bytes 3563528 | tf_op jit(solution)/shard_map/ppermute | solution.py:31
  85.9 8.4 %collective-permute-start.15 = (f32[480]{0:T(512)S(1)}, f32[480]{0:T(512)S(1)}, u32[]{:S(2)}, u32[]{:S(2)}) collective-permute-start(f32[480]{0:T(512)S(1)} %compare_select_fusion.5), channel_id=1, source_target_pairs={{0,1},{1,0},{2,3},{3,2},{4,5},{5,4},{6,7},{7,6},{8,9},{9,8},{10,11... | collective-permute-start | bytes 5768 | tf_op jit(solution)/shard_map/ppermute | solution.py:31
  89.5 5.0 %collective-permute-start.18 = (bf16[160,3712]{1,0:T(8,128)(2,1)S(1)}, bf16[160,3712]{1,0:T(8,128)(2,1)S(1)}, u32[]{:S(2)}, u32[]{:S(2)}) collective-permute-start(bf16[160,3712]{1,0:T(8,128)(2,1)S(1)} %shard_map.131), channel_id=1, source_target_pairs={{0,1},{1,0},{2,3},{3,2},{4,5},{5,4},{6,7},{7,6},{8,9},{9,8},{10,11... | collective-permute-start | bytes 3563528 | tf_op jit(solution)/shard_map/ppermute | solution.py:31
  94.2 6.9 %collective-permute-start.14 = (bf16[480,1792]{1,0:T(8,128)(2,1)}, bf16[480,1792]{1,0:T(8,128)(2,1)}, u32[]{:S(2)}, u32[]{:S(2)}) collective-permute-start(bf16[480,1792]{1,0:T(8,128)(2,1)} %fusion.17), channel_id=1, source_target_pairs={{0,1},{1,0},{2,3},{3,2},{4,5},{5,4},{6,7},{7,6},{8,9},{9,8},{10,11... | collective-permute-start | bytes 5160968 | tf_op jit(solution)/shard_map/ppermute | solution.py:31
  98.1 2.9 %collective-permute-start.20 = (f32[160]{0:T(256)S(1)}, f32[160]{0:T(256)S(1)}, u32[]{:S(2)}, u32[]{:S(2)}) collective-permute-start(f32[160]{0:T(256)S(1)} %compare_select_fusion.4), channel_id=1, source_target_pairs={{0,1},{1,0},{2,3},{3,2},{4,5},{5,4},{6,7},{7,6},{8,9},{9,8},{10,11... | collective-permute-start | bytes 1928 | tf_op jit(solution)/shard_map/ppermute | solution.py:31
  100.9 3.9 %collective-permute-start.19 = (bf16[160,1792]{1,0:T(8,128)(2,1)S(1)}, bf16[160,1792]{1,0:T(8,128)(2,1)S(1)}, u32[]{:S(2)}, u32[]{:S(2)}) collective-permute-start(bf16[160,1792]{1,0:T(8,128)(2,1)S(1)} %fusion.22), channel_id=1, source_target_pairs={{0,1},{1,0},{2,3},{3,2},{4,5},{5,4},{6,7},{7,6},{8,9},{9,8},{10,11... | collective-permute-start | bytes 1720328 | tf_op jit(solution)/shard_map/ppermute | solution.py:31
  106.1 16.6 %collective-permute-start.23 = (bf16[160,1920]{1,0:T(8,128)(2,1)S(1)}, bf16[160,1920]{1,0:T(8,128)(2,1)S(1)}, u32[]{:S(2)}, u32[]{:S(2)}) collective-permute-start(bf16[160,1920]{1,0:T(8,128)(2,1)S(1)} %pad_maximum_fusion.4), channel_id=1, source_target_pairs={{0,4},{1,5},{2,6},{3,7},{4,0},{5,1},{6,2},{7,3},{8,12},{9,13},{10,... | collective-permute-start | bytes 1843208 | tf_op jit(solution)/shard_map/ppermute | solution.py:27
  106.8 26.6 %collective-permute-start.21 = (bf16[160,1920]{1,0:T(8,128)(2,1)S(1)}, bf16[160,1920]{1,0:T(8,128)(2,1)S(1)}, u32[]{:S(2)}, u32[]{:S(2)}) collective-permute-start(bf16[160,1920]{1,0:T(8,128)(2,1)S(1)} %get-tuple-element.56), channel_id=1, source_target_pairs={{0,6},{1,7},{2,0},{3,1},{4,2},{5,3},{6,4},{7,5},{8,14},{9,15},{10,... | collective-permute-start | bytes 1843208 | tf_op jit(solution)/shard_map/ppermute | solution.py:27
  108.9 27.7 %collective-permute-start.22 = (bf16[160,1920]{1,0:T(8,128)(2,1)S(1)}, bf16[160,1920]{1,0:T(8,128)(2,1)S(1)}, u32[]{:S(2)}, u32[]{:S(2)}) collective-permute-start(bf16[160,1920]{1,0:T(8,128)(2,1)S(1)} %get-tuple-element.57), channel_id=1, source_target_pairs={{0,2},{1,3},{2,4},{3,5},{4,6},{5,7},{6,0},{7,1},{8,10},{9,11},{10,... | collective-permute-start | bytes 1843208 | tf_op jit(solution)/shard_map/ppermute | solution.py:27
  137.0 9.8 %collective-permute-start.26 = (bf16[40,1920]{1,0:T(8,128)(2,1)S(1)}, bf16[40,1920]{1,0:T(8,128)(2,1)S(1)}, u32[]{:S(2)}, u32[]{:S(2)}) collective-permute-start(bf16[40,1920]{1,0:T(8,128)(2,1)S(1)} %get-tuple-element.85), channel_id=1, source_target_pairs={{0,8},{8,16},{16,24},{24,0},{32,40},{40,48},{48,56},{56,32},{64,72... | collective-permute-start | bytes 460808 | tf_op jit(solution)/shard_map/ppermute | solution.py:22
  137.1 9.7 %collective-permute-start.25 = (bf16[40,1920]{1,0:T(8,128)(2,1)S(1)}, bf16[40,1920]{1,0:T(8,128)(2,1)S(1)}, u32[]{:S(2)}, u32[]{:S(2)}) collective-permute-start(bf16[40,1920]{1,0:T(8,128)(2,1)S(1)} %get-tuple-element.86), channel_id=1, source_target_pairs={{0,16},{8,24},{16,0},{24,8},{32,48},{40,56},{48,32},{56,40},{64,80... | collective-permute-start | bytes 460808 | tf_op jit(solution)/shard_map/ppermute | solution.py:22
  137.9 9.1 %collective-permute-start.24 = (bf16[40,1920]{1,0:T(8,128)(2,1)S(1)}, bf16[40,1920]{1,0:T(8,128)(2,1)S(1)}, u32[]{:S(2)}, u32[]{:S(2)}) collective-permute-start(bf16[40,1920]{1,0:T(8,128)(2,1)S(1)} %get-tuple-element.87), channel_id=1, source_target_pairs={{0,24},{8,0},{16,8},{24,16},{32,56},{40,32},{48,40},{56,48},{64,88... | collective-permute-start | bytes 460808 | tf_op jit(solution)/shard_map/ppermute | solution.py:22
  147.4 9.9 %collective-permute-start.27 = (bf16[32,1920]{1,0:T(8,128)(2,1)S(1)}, bf16[32,1920]{1,0:T(8,128)(2,1)S(1)}, u32[]{:S(2)}, u32[]{:S(2)}) collective-permute-start(bf16[32,1920]{1,0:T(8,128)(2,1)S(1)} %get-tuple-element.88), channel_id=1, source_target_pairs={{0,96},{8,104},{16,112},{24,120},{32,0},{40,8},{48,16},{56,24},{64... | collective-permute-start | bytes 368648 | tf_op jit(solution)/shard_map/ppermute | solution.py:17
  150.4 6.8 %collective-permute-start.29 = (bf16[32,1920]{1,0:T(8,128)(2,1)S(1)}, bf16[32,1920]{1,0:T(8,128)(2,1)S(1)}, u32[]{:S(2)}, u32[]{:S(2)}) collective-permute-start(bf16[32,1920]{1,0:T(8,128)(2,1)S(1)} %get-tuple-element.89), channel_id=1, source_target_pairs={{0,64},{8,72},{16,80},{24,88},{32,96},{40,104},{48,112},{56,120},{... | collective-permute-start | bytes 368648 | tf_op jit(solution)/shard_map/ppermute | solution.py:17
  150.6 6.7 %collective-permute-start.28 = (bf16[32,1920]{1,0:T(8,128)(2,1)S(1)}, bf16[32,1920]{1,0:T(8,128)(2,1)S(1)}, u32[]{:S(2)}, u32[]{:S(2)}) collective-permute-start(bf16[32,1920]{1,0:T(8,128)(2,1)S(1)} %get-tuple-element.90), channel_id=1, source_target_pairs={{0,32},{8,40},{16,48},{24,56},{32,64},{40,72},{48,80},{56,88},{64,... | collective-permute-start | bytes 368648 | tf_op jit(solution)/shard_map/ppermute | solution.py:17
  157.4 3.9 %collective-permute-start.30 = (bf16[16,1792]{1,0:T(8,128)(2,1)S(1)}, bf16[16,1792]{1,0:T(8,128)(2,1)S(1)}, u32[]{:S(2)}, u32[]{:S(2)}) collective-permute-start(bf16[16,1792]{1,0:T(8,128)(2,1)S(1)} %slice.144), channel_id=1, source_target_pairs={{0,1},{1,0},{2,3},{3,2},{4,5},{5,4},{6,7},{7,6},{8,9},{9,8},{10,11... | collective-permute-start | bytes 172040 | tf_op jit(solution)/shard_map/ppermute | solution.py:31

commit v3 on v2

--- a/solution.py
+++ b/solution.py
@@ -246,18 +246,21 @@
     far_state, far_full = row_gradients(far, across(far))
 
     near_full, far_full = lax.optimization_barrier((near_full, far_full))
-    own_rows, below_rows, above_rows = jnp.split(near_full, 3, axis=0)
-    back_parts = [
-        own_rows,
-        along_y(below_rows, -1),
-        along_y(above_rows, 1),
-        along_y(far_full, 2),
-    ]
+    own_top, own_bottom, below_top, below_bottom, above_top, above_bottom = jnp.split(
+        near_full, 6, axis=0
+    )
+    from_above = along_y(jnp.concatenate([far_full[:side], below_bottom], axis=0), -1)
+    from_below = along_y(jnp.concatenate([far_full[side:], above_top], axis=0), 1)
+    early_top, early_bottom = from_below[side:], from_above[side:]
+    late_top = along_y(below_top + from_above[:side], -1)
+    late_bottom = along_y(above_bottom + from_below[:side], 1)
 
     def add(*parts):
         return sum(p.astype(F32) for p in parts).astype(BF)
 
-    back = jnp.split(add(*back_parts), 4, axis=0)
+    top_rows = add(own_top, early_top, late_top)
+    bottom_rows = add(own_bottom, early_bottom, late_bottom)
+    back = [top_rows[:slots], top_rows[slots:], bottom_rows[:slots], bottom_rows[slots:]]
     back = jnp.concatenate(exchange_z(back, -1), axis=0)
     parts = jnp.split(tn(select, back).astype(BF), 4, axis=0)
     parts = [parts[0], along_x(parts[1], -1), along_x(parts[2], 1), along_x(parts[3], 2)]

time: 162 us -> 157 us (0.969)
  waiting for transfers between devices: 63.1 us -> 55.9 us
  starting transfers between devices: 36.8 us -> 40.2 us
    ppermute x9 -> x10, waiting for transfers between devices: 44.1 us -> 37.5 us  [along_y(): return lax.ppermute(value, 'local', pairs)]
    ppermute x9 -> x10, starting transfers between devices: 9.8 us -> 12.4 us  [along_y(): return lax.ppermute(value, 'local', pairs)]
    ppermute x10, starting transfers between devices: 10.8 us -> 12.7 us  [across(): return lax.ppermute(value, 'local', [(i, i ^ 1) for i in range(8)])]
  transfers between devices with their start and end apart: 31 -> 32, of which waited for: 14 -> 11; matrix products, arithmetic and copies ran while one was open for 29% -> 29% of each run, Pallas kernels for 1% -> 1%
where the time goes in v3:
time: 157 us
  waiting for transfers between devices  55.9 us (36%)
  starting transfers between devices  40.2 us (26%)
  matrix products  38.5 us (25%)
  local copies, waits for them, and re-layouts  11.8 us (8%)
  other arithmetic  5.86 us (4%)
  Pallas kernels  3.5 us (2%)
    dot_general x19, matrix products, dot(): lax.dot_general(left, right, ((dims[0], dims[1]), ((), ())), preferred_el...  38.5 us
    ppermute x10, waiting for transfers between devices, along_y(): return lax.ppermute(value, 'local', pairs)  37.5 us
    ppermute x10, starting transfers between devices, across(): return lax.ppermute(value, 'local', [(i, i ^ 1) for i in range(8)])  12.7 us
    ppermute x10, starting transfers between devices, along_y(): return lax.ppermute(value, 'local', pairs)  12.4 us
    unnamed x25, local copies, waits for them, and re-layouts  10.4 us
    ppermute x6, waiting for transfers between devices, along_x(): return lax.ppermute(value, 'node', pairs)  9.1 us
    ppermute x6, starting transfers between devices, along_x(): return lax.ppermute(value, 'node', pairs)  8.63 us
    ppermute x6, waiting for transfers between devices, along_z(): return lax.ppermute(value, 'node', pairs)  7.75 us
  transfers between devices with their start and end apart: 32, of which 11 were waited for; matrix products, arithmetic and copies ran while one was open for 29% of the time, Pallas kernels for 1%

profile of v3, /device:TPU:1, one launch (start us, length us, event | category | flops | bytes accessed | tf_op | source)
XLA Modules:
  0.0 156.9 jit_solution(7909662897601080631)
XLA Ops:
  0.6 1.9 %shard_map.128 = (bf16[16,3712]{1,0:T(8,128)(2,1)}, bf16[16,3712]{1,0:T(8,128)(2,1)}) custom-call(s32[1]{0:T(128)} %bitcast.core, bf16[16,3584]{1,0:T(8,128)(2,1)} %tok.1, bf16[16,3584]{1,0:T(8,128)(2,1)} %cot.1, s32[4,16]{1,0:T(4,128)} %bitcast.38, s32[1,16]{1,0:T(1,128)} %homes.1, s32[4,16]{1,0:T(4,128)} %bitcast.40, bf16[8,16]{1,0:T(8,128)(2,1)} %bitcast.41), custom_call_target="tpu_custom_call" | custom-call | tf_op jit(solution)/shard_map/pallas_call | solution.py:148
  2.5 1.4 collective-permute-start
  3.9 0.7 broadcast_multiply_fusion.2
  4.6 0.9 constant_dynamic-update-slice_fusion.1
  5.6 0.9 select_reduce_fusion.3
  6.5 1.4 collective-permute-start.1
  8.0 0.7 fusion.75
  8.7 2.5 %collective-permute-start.3 = (bf16[32,3712]{1,0:T(8,128)(2,1)S(1)}, bf16[32,3712]{1,0:T(8,128)(2,1)S(1)}, u32[]{:S(2)}, u32[]{:S(2)}) collective-permute-start(bf16[32,3712]{1,0:T(8,128)(2,1)S(1)} %get-tuple-element.107), channel_id=1, source_target_pairs={{0,64},{8,72},{16,80},{24,88},{32,96},{40,104},{48,112},{56,120},{... | collective-permute-start | bytes 712712 | tf_op jit(solution)/shard_map/ppermute | solution.py:17
  11.2 1.2 collective-permute-start.2
  12.3 2.9 %collective-permute-done.1 = bf16[32,3712]{1,0:T(8,128)(2,1)S(1)} collective-permute-done((bf16[32,3712]{1,0:T(8,128)(2,1)S(1)}, bf16[32,3712]{1,0:T(8,128)(2,1)S(1)}, u32[]{:S(2)}, u32[]{:S(2)}) %collective-permute-start.1) | collective-permute-done | bytes 237600 | tf_op jit(solution)/shard_map/ppermute | solution.py:17
  15.3 6.2 %collective-permute-done.2 = bf16[32,3712]{1,0:T(8,128)(2,1)S(1)} collective-permute-done((bf16[32,3712]{1,0:T(8,128)(2,1)S(1)}, bf16[32,3712]{1,0:T(8,128)(2,1)S(1)}, u32[]{:S(2)}, u32[]{:S(2)}) %collective-permute-start.2) | collective-permute-done | bytes 237600 | tf_op jit(solution)/shard_map/ppermute | solution.py:17
  22.1 0.5 convolution_convert_fusion.3
  22.5 0.9 constant_dynamic-update-slice_fusion.24
  23.5 2.8 %collective-permute-start.8 = (bf16[40,3712]{1,0:T(8,128)(2,1)S(1)}, bf16[40,3712]{1,0:T(8,128)(2,1)S(1)}, u32[]{:S(2)}, u32[]{:S(2)}) collective-permute-start(bf16[40,3712]{1,0:T(8,128)(2,1)S(1)} %get-tuple-element.67), channel_id=1, source_target_pairs={{0,6},{1,7},{2,0},{3,1},{4,2},{5,3},{6,4},{7,5},{8,14},{9,15},{10,... | collective-permute-start | bytes 890888 | tf_op jit(solution)/shard_map/ppermute | solution.py:27
  26.3 3.8 %collective-permute-start.6 = (bf16[40,3712]{1,0:T(8,128)(2,1)S(1)}, bf16[40,3712]{1,0:T(8,128)(2,1)S(1)}, u32[]{:S(2)}, u32[]{:S(2)}) collective-permute-start(bf16[40,3712]{1,0:T(8,128)(2,1)S(1)} %get-tuple-element.64), channel_id=1, source_target_pairs={{0,24},{8,0},{16,8},{24,16},{32,56},{40,32},{48,40},{56,48},{64,88... | collective-permute-start | bytes 890888 | tf_op jit(solution)/shard_map/ppermute | solution.py:22
  30.0 0.7 collective-permute-start.4
  30.8 2.0 %copy-done = bf16[1,3584,512]{2,1,0:T(8,128)(2,1)S(1)} copy-done((bf16[1,3584,512]{2,1,0:T(8,128)(2,1)S(1)}, bf16[1,3584,512]{2,1,0:T(8,128)(2,1)}, u32[]{:S(2)}) %copy-start) | copy-done | bytes 3670040
  32.9 2.0 %copy-done.1 = bf16[1,3584,512]{2,1,0:T(8,128)(2,1)S(1)} copy-done((bf16[1,3584,512]{2,1,0:T(8,128)(2,1)S(1)}, bf16[1,3584,512]{2,1,0:T(8,128)(2,1)}, u32[]{:S(2)}) %copy-start.1) | copy-done | bytes 3670040
  34.9 2.0 %copy-done.2 = bf16[1,512,3584]{2,1,0:T(8,128)(2,1)S(1)} copy-done((bf16[1,512,3584]{2,1,0:T(8,128)(2,1)S(1)}, bf16[1,512,3584]{2,1,0:T(8,128)(2,1)}, u32[]{:S(2)}) %copy-start.2) | copy-done | bytes 3670040
  36.9 1.5 shard_map.130
  38.5 2.7 %collective-permute-done.6.refs_2_ = bf16[40,3712]{1,0:T(8,128)(2,1)S(1)} collective-permute-done((bf16[40,3712]{1,0:T(8,128)(2,1)S(1)}, bf16[40,3712]{1,0:T(8,128)(2,1)S(1)}, u32[]{:S(2)}, u32[]{:S(2)}) %collective-permute-start.6) | collective-permute-done | bytes 296992 | tf_op jit(solution)/shard_map/ppermute | solution.py:22
  41.2 5.0 %collective-permute-done.4.refs_0_ = bf16[40,3712]{1,0:T(8,128)(2,1)S(1)} collective-permute-done((bf16[40,3712]{1,0:T(8,128)(2,1)S(1)}, bf16[40,3712]{1,0:T(8,128)(2,1)S(1)}, u32[]{:S(2)}, u32[]{:S(2)}) %collective-permute-start.4) | collective-permute-done | bytes 296992 | tf_op jit(solution)/shard_map/ppermute | solution.py:22
  46.4 2.7 %collective-permute-start.10 = (bf16[120,3712]{1,0:T(8,128)(2,1)S(1)}, bf16[120,3712]{1,0:T(8,128)(2,1)S(1)}, u32[]{:S(2)}, u32[]{:S(2)}) collective-permute-start(bf16[120,3712]{1,0:T(8,128)(2,1)S(1)} %shard_map.129), channel_id=1, source_target_pairs={{0,6},{1,7},{2,0},{3,1},{4,2},{5,3},{6,4},{7,5},{8,14},{9,15},{10,... | collective-permute-start | bytes 2672648 | tf_op jit(solution)/shard_map/ppermute | solution.py:27
  49.1 1.1 collective-permute-start.11
  50.6 19.9 %collective-permute-done.9 = bf16[120,3712]{1,0:T(8,128)(2,1)S(1)} collective-permute-done((bf16[120,3712]{1,0:T(8,128)(2,1)S(1)}, bf16[120,3712]{1,0:T(8,128)(2,1)S(1)}, u32[]{:S(2)}, u32[]{:S(2)}) %collective-permute-start.9) | collective-permute-done | bytes 890912 | tf_op jit(solution)/shard_map/ppermute | solution.py:27
  70.5 0.3 constant_dynamic-update-slice_fusion.21
  70.9 2.1 %collective-permute-start.12 = (bf16[160,3712]{1,0:T(8,128)(2,1)S(1)}, bf16[160,3712]{1,0:T(8,128)(2,1)S(1)}, u32[]{:S(2)}, u32[]{:S(2)}) collective-permute-start(bf16[160,3712]{1,0:T(8,128)(2,1)S(1)} %get-tuple-element.80), channel_id=1, source_target_pairs={{0,1},{1,0},{2,3},{3,2},{4,5},{5,4},{6,7},{7,6},{8,9},{9,8},{10,11... | collective-permute-start | bytes 3563528 | tf_op jit(solution)/shard_map/ppermute | solution.py:31
  73.2 1.5 collective-permute-start.16
  74.7 0.8 collective-permute-start.13
  76.2 0.3 constant_dynamic-update-slice_fusion.27
  76.5 1.6 collective-permute-done.13
  78.3 1.1 fusion.29
  79.4 2.3 %fusion.25 = f32[480,1024]{1,0:T(8,128)S(1)} fusion(bf16[1920,1024]{1,0:T(8,128)(2,1)S(1)} %get-tuple-element.26, bf16[480,3712]{1,0:T(8,128)(2,1)S(1)} %get-tuple-element.69), kind=kOutput, calls=%fused_computation.27 | convolution fusion | flops 1887436800 | bytes 7741440 | tf_op jit(solution)/shard_map/dot_general | solution.py:35
  81.7 2.3 %fusion.33 = f32[480,1024]{1,0:T(8,128)S(1)} fusion(f32[480,1024]{1,0:T(8,128)S(1)} %fusion.25, bf16[1920,1024]{1,0:T(8,128)(2,1)S(1)} %get-tuple-element.25, bf16[480,3712]{1,0:T(8,128)(2,1)S(1)} %get-tuple-element.78), kind=kOutput, calls=%fused_computation.36 | convolution fusion | flops 1887928320 | bytes 9707520 | tf_op jit(solution)/shard_map/dot_general | solution.py:35
  84.0 0.6 broadcast_multiply_fusion
  84.5 1.3 multiply_convert_fusion.1
  85.9 0.5 collective-permute-start.15
  86.5 1.7 %collective-permute-done.17.refs_1_ = bf16[80,3712]{1,0:T(8,128)(2,1)S(1)} collective-permute-done((bf16[80,3712]{1,0:T(8,128)(2,1)S(1)}, bf16[80,3712]{1,0:T(8,128)(2,1)S(1)}, u32[]{:S(2)}, u32[]{:S(2)}) %collective-permute-start.17) | collective-permute-done | bytes 593952 | tf_op jit(solution)/shard_map/ppermute | solution.py:27
  88.2 1.3 collective-permute-done.16.refs_0_
  89.5 0.9 collective-permute-start.18
  90.9 3.2 %fusion.17 = bf16[480,1792]{1,0:T(8,128)(2,1)} fusion(bf16[1920,1024]{1,0:T(8,128)(2,1)S(1)} %get-tuple-element.26, bf16[480,512]{1,0:T(8,128)(2,1)S(1)} %get-tuple-element.76, bf16[480,512]{1,0:T(8,128)(2,1)S(1)} %get-tuple-element.74), kind=kOutput, calls=%fused_computation.24 | convolution fusion | flops 1764433920 | bytes 6373376 | tf_op jit(solution)/shard_map/dot_general | solution.py:35
  94.5 0.8 fusion.47
  95.4 0.9 convolution_add_fusion
  96.4 0.7 fusion.57
  97.2 0.9 multiply_convert_fusion.5
  98.1 0.8 collective-permute-start.20
  98.9 1.3 fusion.22
  100.8 2.0 %add_convert_fusion = bf16[480,1792]{1,0:T(8,128)(2,1)S(1)} fusion(bf16[480,1792]{1,0:T(8,128)(2,1)S(1)} %collective-permute-done.14, bf16[1920,1024]{1,0:T(8,128)(2,1)S(1)} %get-tuple-element.25, bf16[480,512]{1,0:T(8,128)(2,1)S(1)} %get-tuple-element.76, bf16[480,512]{1,0:T(8,128)(2,1)S(1)} %get-tuple-element.74), kind=kOutput, calls=%fused_computation.15 | convolution fusion | flops 1766154240 | bytes 8093696 | tf_op jit(solution)/shard_map/dot_general | solution.py:35
  103.0 1.4 add_convert_fusion.1
  104.8 2.6 %collective-permute-start.22 = (bf16[160,1920]{1,0:T(8,128)(2,1)S(1)}, bf16[160,1920]{1,0:T(8,128)(2,1)S(1)}, u32[]{:S(2)}, u32[]{:S(2)}) collective-permute-start(bf16[160,1920]{1,0:T(8,128)(2,1)S(1)} %pad_maximum_fusion.6), channel_id=1, source_target_pairs={{0,6},{1,7},{2,0},{3,1},{4,2},{5,3},{6,4},{7,5},{8,14},{9,15},{10,... | collective-permute-start | bytes 1843208 | tf_op jit(solution)/shard_map/ppermute | solution.py:27
  107.7 13.1 %collective-permute-done.21 = bf16[160,1920]{1,0:T(8,128)(2,1)S(1)} collective-permute-done((bf16[160,1920]{1,0:T(8,128)(2,1)S(1)}, bf16[160,1920]{1,0:T(8,128)(2,1)S(1)}, u32[]{:S(2)}, u32[]{:S(2)}) %collective-permute-start.21) | collective-permute-done | bytes 614432 | tf_op jit(solution)/shard_map/ppermute | solution.py:27
  120.9 2.5 %collective-permute-start.23 = (bf16[80,1920]{1,0:T(8,128)(2,1)S(1)}, bf16[80,1920]{1,0:T(8,128)(2,1)S(1)}, u32[]{:S(2)}, u32[]{:S(2)}) collective-permute-start(bf16[80,1920]{1,0:T(8,128)(2,1)S(1)} %get-tuple-element.58), channel_id=1, source_target_pairs={{0,6},{1,7},{2,0},{3,1},{4,2},{5,3},{6,4},{7,5},{8,14},{9,15},{10,... | collective-permute-start | bytes 921608 | tf_op jit(solution)/shard_map/ppermute | solution.py:27
  123.4 6.6 %fusion.1 = bf16[1,3584,512]{2,1,0:T(8,128)(2,1)} fusion(bf16[640,1792]{1,0:T(8,128)(2,1)S(1)} %get-tuple-element.51, bf16[640,1792]{1,0:T(8,128)(2,1)S(1)} %get-tuple-element.49, pred[]{:T(512)S(6)} %eq.114, bf16[640,1024]{1,0:T(8,128)(2,1)S(1)} %maximum_maximum_fusion), kind=kOutput, calls=%fused_computation.4 | convolution fusion | flops 2371289088 | bytes 8912897 | tf_op jit(solution)/shard_map/dot_general | solution.py:35
  130.0 1.5 collective-permute-done.25
  131.9 0.7 collective-permute-start.26
  132.6 1.1 collective-permute-start.27
  133.7 6.6 %fusion = bf16[1,3584,512]{2,1,0:T(8,128)(2,1)} fusion(bf16[640,1792]{1,0:T(8,128)(2,1)S(1)} %get-tuple-element.51, bf16[640,1792]{1,0:T(8,128)(2,1)S(1)} %get-tuple-element.49, pred[]{:T(512)S(6)} %eq.114, bf16[640,1024]{1,0:T(8,128)(2,1)S(1)} %maximum_maximum_fusion), kind=kOutput, calls=%fused_computation.3 | convolution fusion | flops 2371289088 | bytes 8912897 | tf_op jit(solution)/shard_map/dot_general | solution.py:35
  140.4 0.4 convolution_convert_fusion.4
  140.8 3.0 %collective-permute-start.28 = (bf16[32,1920]{1,0:T(8,128)(2,1)S(1)}, bf16[32,1920]{1,0:T(8,128)(2,1)S(1)}, u32[]{:S(2)}, u32[]{:S(2)}) collective-permute-start(bf16[32,1920]{1,0:T(8,128)(2,1)S(1)} %get-tuple-element.90), channel_id=1, source_target_pairs={{0,96},{8,104},{16,112},{24,120},{32,0},{40,8},{48,16},{56,24},{64... | collective-permute-start | bytes 368648 | tf_op jit(solution)/shard_map/ppermute | solution.py:17
  144.0 0.4 collective-permute-start.29
  144.4 5.9 %fusion.2 = bf16[1,512,3584]{2,1,0:T(8,128)(2,1)} fusion(bf16[640,1792]{1,0:T(8,128)(2,1)S(1)} %get-tuple-element.50, bf16[640,1792]{1,0:T(8,128)(2,1)S(1)} %get-tuple-element.48, pred[]{:T(512)S(6)} %eq.114, bf16[160,512]{1,0:T(8,128)(2,1)S(1)} %get-tuple-element.36, bf16[480,512]{1,0:T(8,128)(2,1)S(1)} %get-tuple-element.35), kind=kOutput, calls=%fused_computation.5 | convolution fusion | flops 2372599808 | bytes 8912897 | tf_op jit(solution)/shard_map/dot_general | solution.py:35
  150.5 4.8 %collective-permute-start.31 = (bf16[16,1792]{1,0:T(8,128)(2,1)S(1)}, bf16[16,1792]{1,0:T(8,128)(2,1)S(1)}, u32[]{:S(2)}, u32[]{:S(2)}) collective-permute-start(bf16[16,1792]{1,0:T(8,128)(2,1)S(1)} %slice.192), channel_id=1, source_target_pairs={{0,1},{1,0},{2,3},{3,2},{4,5},{5,4},{6,7},{7,6},{8,9},{9,8},{10,11... | collective-permute-start | bytes 172040 | tf_op jit(solution)/shard_map/ppermute | solution.py:31
  155.5 0.7 copy.19
  156.3 0.7 pad_maximum_fusion.12
  (104 shorter events, 6.4 us)
Async XLA Ops:
  2.5 4.0 %collective-permute-start = (bf16[16,3712]{1,0:T(8,128)(2,1)}, bf16[16,3712]{1,0:T(8,128)(2,1)S(1)}, u32[]{:S(2)}, u32[]{:S(2)}) collective-permute-start(bf16[16,3712]{1,0:T(8,128)(2,1)} %get-tuple-element.22._), channel_id=1, source_target_pairs={{0,1},{1,0},{2,3},{3,2},{4,5},{5,4},{6,7},{7,6},{8,9},{9,8},{10,11... | collective-permute-start | bytes 356360 | tf_op jit(solution)/shard_map/ppermute | solution.py:31
  6.5 24.3 %copy-start.3 = (bf16[16,3712]{1,0:T(8,128)(2,1)S(1)}, bf16[16,3712]{1,0:T(8,128)(2,1)}, u32[]{:S(2)}) copy-start(bf16[16,3712]{1,0:T(8,128)(2,1)} %get-tuple-element.22._) | copy-start | bytes 356356
  6.5 8.7 %collective-permute-start.1 = (bf16[32,3712]{1,0:T(8,128)(2,1)S(1)}, bf16[32,3712]{1,0:T(8,128)(2,1)S(1)}, u32[]{:S(2)}, u32[]{:S(2)}) collective-permute-start(bf16[32,3712]{1,0:T(8,128)(2,1)S(1)} %get-tuple-element.107), channel_id=1, source_target_pairs={{0,32},{8,40},{16,48},{24,56},{32,64},{40,72},{48,80},{56,88},{64,... | collective-permute-start | bytes 712712 | tf_op jit(solution)/shard_map/ppermute | solution.py:17
  8.7 12.7 %collective-permute-start.3 = (bf16[32,3712]{1,0:T(8,128)(2,1)S(1)}, bf16[32,3712]{1,0:T(8,128)(2,1)S(1)}, u32[]{:S(2)}, u32[]{:S(2)}) collective-permute-start(bf16[32,3712]{1,0:T(8,128)(2,1)S(1)} %get-tuple-element.107), channel_id=1, source_target_pairs={{0,64},{8,72},{16,80},{24,88},{32,96},{40,104},{48,112},{56,120},{... | collective-permute-start | bytes 712712 | tf_op jit(solution)/shard_map/ppermute | solution.py:17
  11.2 10.3 %collective-permute-start.2 = (bf16[32,3712]{1,0:T(8,128)(2,1)S(1)}, bf16[32,3712]{1,0:T(8,128)(2,1)S(1)}, u32[]{:S(2)}, u32[]{:S(2)}) collective-permute-start(bf16[32,3712]{1,0:T(8,128)(2,1)S(1)} %get-tuple-element.107), channel_id=1, source_target_pairs={{0,96},{8,104},{16,112},{24,120},{32,0},{40,8},{48,16},{56,24},{64... | collective-permute-start | bytes 712712 | tf_op jit(solution)/shard_map/ppermute | solution.py:17
  23.5 22.8 %collective-permute-start.8 = (bf16[40,3712]{1,0:T(8,128)(2,1)S(1)}, bf16[40,3712]{1,0:T(8,128)(2,1)S(1)}, u32[]{:S(2)}, u32[]{:S(2)}) collective-permute-start(bf16[40,3712]{1,0:T(8,128)(2,1)S(1)} %get-tuple-element.67), channel_id=1, source_target_pairs={{0,6},{1,7},{2,0},{3,1},{4,2},{5,3},{6,4},{7,5},{8,14},{9,15},{10,... | collective-permute-start | bytes 890888 | tf_op jit(solution)/shard_map/ppermute | solution.py:27
  26.3 20.0 %collective-permute-start.7 = (bf16[40,3712]{1,0:T(8,128)(2,1)S(1)}, bf16[40,3712]{1,0:T(8,128)(2,1)S(1)}, u32[]{:S(2)}, u32[]{:S(2)}) collective-permute-start(bf16[40,3712]{1,0:T(8,128)(2,1)S(1)} %get-tuple-element.67), channel_id=1, source_target_pairs={{0,2},{1,3},{2,4},{3,5},{4,6},{5,7},{6,0},{7,1},{8,10},{9,11},{10,... | collective-permute-start | bytes 890888 | tf_op jit(solution)/shard_map/ppermute | solution.py:27
  26.3 14.9 %collective-permute-start.6 = (bf16[40,3712]{1,0:T(8,128)(2,1)S(1)}, bf16[40,3712]{1,0:T(8,128)(2,1)S(1)}, u32[]{:S(2)}, u32[]{:S(2)}) collective-permute-start(bf16[40,3712]{1,0:T(8,128)(2,1)S(1)} %get-tuple-element.64), channel_id=1, source_target_pairs={{0,24},{8,0},{16,8},{24,16},{32,56},{40,32},{48,40},{56,48},{64,88... | collective-permute-start | bytes 890888 | tf_op jit(solution)/shard_map/ppermute | solution.py:22
  30.0 11.2 %collective-permute-start.5 = (bf16[40,3712]{1,0:T(8,128)(2,1)S(1)}, bf16[40,3712]{1,0:T(8,128)(2,1)S(1)}, u32[]{:S(2)}, u32[]{:S(2)}) collective-permute-start(bf16[40,3712]{1,0:T(8,128)(2,1)S(1)} %get-tuple-element.65), channel_id=1, source_target_pairs={{0,16},{8,24},{16,0},{24,8},{32,48},{40,56},{48,32},{56,40},{64,80... | collective-permute-start | bytes 890888 | tf_op jit(solution)/shard_map/ppermute | solution.py:22
  30.0 16.2 %collective-permute-start.4 = (bf16[40,3712]{1,0:T(8,128)(2,1)S(1)}, bf16[40,3712]{1,0:T(8,128)(2,1)S(1)}, u32[]{:S(2)}, u32[]{:S(2)}) collective-permute-start(bf16[40,3712]{1,0:T(8,128)(2,1)S(1)} %get-tuple-element.66), channel_id=1, source_target_pairs={{0,8},{8,16},{16,24},{24,0},{32,40},{40,48},{48,56},{56,32},{64,72... | collective-permute-start | bytes 890888 | tf_op jit(solution)/shard_map/ppermute | solution.py:22
  30.8 2.0 %copy-start = (bf16[1,3584,512]{2,1,0:T(8,128)(2,1)S(1)}, bf16[1,3584,512]{2,1,0:T(8,128)(2,1)}, u32[]{:S(2)}) copy-start(bf16[1,3584,512]{2,1,0:T(8,128)(2,1)} %param.15) | copy-start | bytes 11010052
  32.9 2.0 %copy-start.1 = (bf16[1,3584,512]{2,1,0:T(8,128)(2,1)S(1)}, bf16[1,3584,512]{2,1,0:T(8,128)(2,1)}, u32[]{:S(2)}) copy-start(bf16[1,3584,512]{2,1,0:T(8,128)(2,1)} %param.16) | copy-start | bytes 11010052
  34.9 2.0 %copy-start.2 = (bf16[1,512,3584]{2,1,0:T(8,128)(2,1)S(1)}, bf16[1,512,3584]{2,1,0:T(8,128)(2,1)}, u32[]{:S(2)}) copy-start(bf16[1,512,3584]{2,1,0:T(8,128)(2,1)} %param.17) | copy-start | bytes 11010052
  36.9 13.3 %copy-start.5 = (bf16[480,3712]{1,0:T(8,128)(2,1)S(1)}, bf16[480,3712]{1,0:T(8,128)(2,1)}, u32[]{:S(2)}) copy-start(bf16[480,3712]{1,0:T(8,128)(2,1)} %get-tuple-element.63) | copy-start | bytes 10690564
  38.5 11.8 %copy-start.4 = (bf16[640,3712]{1,0:T(8,128)(2,1)S(1)}, bf16[640,3712]{1,0:T(8,128)(2,1)}, u32[]{:S(2)}) copy-start(bf16[640,3712]{1,0:T(8,128)(2,1)} %get-tuple-element.62) | copy-start | bytes 14254084
  46.4 26.6 %collective-permute-start.10 = (bf16[120,3712]{1,0:T(8,128)(2,1)S(1)}, bf16[120,3712]{1,0:T(8,128)(2,1)S(1)}, u32[]{:S(2)}, u32[]{:S(2)}) collective-permute-start(bf16[120,3712]{1,0:T(8,128)(2,1)S(1)} %shard_map.129), channel_id=1, source_target_pairs={{0,6},{1,7},{2,0},{3,1},{4,2},{5,3},{6,4},{7,5},{8,14},{9,15},{10,... | collective-permute-start | bytes 2672648 | tf_op jit(solution)/shard_map/ppermute | solution.py:27
  49.1 21.4 %collective-permute-start.9 = (bf16[120,3712]{1,0:T(8,128)(2,1)S(1)}, bf16[120,3712]{1,0:T(8,128)(2,1)S(1)}, u32[]{:S(2)}, u32[]{:S(2)}) collective-permute-start(bf16[120,3712]{1,0:T(8,128)(2,1)S(1)} %shard_map.129), channel_id=1, source_target_pairs={{0,2},{1,3},{2,4},{3,5},{4,6},{5,7},{6,0},{7,1},{8,10},{9,11},{10,... | collective-permute-start | bytes 2672648 | tf_op jit(solution)/shard_map/ppermute | solution.py:27
  49.1 26.8 %collective-permute-start.11 = (bf16[160,3712]{1,0:T(8,128)(2,1)S(1)}, bf16[160,3712]{1,0:T(8,128)(2,1)S(1)}, u32[]{:S(2)}, u32[]{:S(2)}) collective-permute-start(bf16[160,3712]{1,0:T(8,128)(2,1)S(1)} %pad_maximum_fusion.1), channel_id=1, source_target_pairs={{0,1},{1,0},{2,3},{3,2},{4,5},{5,4},{6,7},{7,6},{8,9},{9,8},{10,11... | collective-permute-start | bytes 3563528 | tf_op jit(solution)/shard_map/ppermute | solution.py:31
  70.9 5.3 %collective-permute-start.12 = (bf16[160,3712]{1,0:T(8,128)(2,1)S(1)}, bf16[160,3712]{1,0:T(8,128)(2,1)S(1)}, u32[]{:S(2)}, u32[]{:S(2)}) collective-permute-start(bf16[160,3712]{1,0:T(8,128)(2,1)S(1)} %get-tuple-element.80), channel_id=1, source_target_pairs={{0,1},{1,0},{2,3},{3,2},{4,5},{5,4},{6,7},{7,6},{8,9},{9,8},{10,11... | collective-permute-start | bytes 3563528 | tf_op jit(solution)/shard_map/ppermute | solution.py:31
  73.1 15.1 %collective-permute-start.17 = (bf16[80,3712]{1,0:T(8,128)(2,1)S(1)}, bf16[80,3712]{1,0:T(8,128)(2,1)S(1)}, u32[]{:S(2)}, u32[]{:S(2)}) collective-permute-start(bf16[80,3712]{1,0:T(8,128)(2,1)S(1)} %slice.175), channel_id=1, source_target_pairs={{0,6},{1,7},{2,0},{3,1},{4,2},{5,3},{6,4},{7,5},{8,14},{9,15},{10,... | collective-permute-start | bytes 1781768 | tf_op jit(solution)/shard_map/ppermute | solution.py:27
  73.2 16.3 %collective-permute-start.16 = (bf16[80,3712]{1,0:T(8,128)(2,1)S(1)}, bf16[80,3712]{1,0:T(8,128)(2,1)S(1)}, u32[]{:S(2)}, u32[]{:S(2)}) collective-permute-start(bf16[80,3712]{1,0:T(8,128)(2,1)S(1)} %slice.174), channel_id=1, source_target_pairs={{0,2},{1,3},{2,4},{3,5},{4,6},{5,7},{6,0},{7,1},{8,10},{9,11},{10,... | collective-permute-start | bytes 1781768 | tf_op jit(solution)/shard_map/ppermute | solution.py:27
  74.7 3.3 %collective-permute-start.13 = (bf16[160,3712]{1,0:T(8,128)(2,1)S(1)}, bf16[160,3712]{1,0:T(8,128)(2,1)S(1)}, u32[]{:S(2)}, u32[]{:S(2)}) collective-permute-start(bf16[160,3712]{1,0:T(8,128)(2,1)S(1)} %pad_maximum_fusion.2), channel_id=1, source_target_pairs={{0,1},{1,0},{2,3},{3,2},{4,5},{5,4},{6,7},{7,6},{8,9},{9,8},{10,11... | collective-permute-start | bytes 3563528 | tf_op jit(solution)/shard_map/ppermute | solution.py:31
  85.9 8.4 %collective-permute-start.15 = (f32[480]{0:T(512)S(1)}, f32[480]{0:T(512)S(1)}, u32[]{:S(2)}, u32[]{:S(2)}) collective-permute-start(f32[480]{0:T(512)S(1)} %compare_select_fusion.5), channel_id=1, source_target_pairs={{0,1},{1,0},{2,3},{3,2},{4,5},{5,4},{6,7},{7,6},{8,9},{9,8},{10,11... | collective-permute-start | bytes 5768 | tf_op jit(solution)/shard_map/ppermute | solution.py:31
  89.5 5.0 %collective-permute-start.18 = (bf16[160,3712]{1,0:T(8,128)(2,1)S(1)}, bf16[160,3712]{1,0:T(8,128)(2,1)S(1)}, u32[]{:S(2)}, u32[]{:S(2)}) collective-permute-start(bf16[160,3712]{1,0:T(8,128)(2,1)S(1)} %shard_map.131), channel_id=1, source_target_pairs={{0,1},{1,0},{2,3},{3,2},{4,5},{5,4},{6,7},{7,6},{8,9},{9,8},{10,11... | collective-permute-start | bytes 3563528 | tf_op jit(solution)/shard_map/ppermute | solution.py:31
  94.2 6.6 %collective-permute-start.14 = (bf16[480,1792]{1,0:T(8,128)(2,1)}, bf16[480,1792]{1,0:T(8,128)(2,1)S(1)}, u32[]{:S(2)}, u32[]{:S(2)}) collective-permute-start(bf16[480,1792]{1,0:T(8,128)(2,1)} %fusion.17), channel_id=1, source_target_pairs={{0,1},{1,0},{2,3},{3,2},{4,5},{5,4},{6,7},{7,6},{8,9},{9,8},{10,11... | collective-permute-start | bytes 5160968 | tf_op jit(solution)/shard_map/ppermute | solution.py:31
  98.1 2.6 %collective-permute-start.20 = (f32[160]{0:T(256)S(1)}, f32[160]{0:T(256)S(1)}, u32[]{:S(2)}, u32[]{:S(2)}) collective-permute-start(f32[160]{0:T(256)S(1)} %compare_select_fusion.4), channel_id=1, source_target_pairs={{0,1},{1,0},{2,3},{3,2},{4,5},{5,4},{6,7},{7,6},{8,9},{9,8},{10,11... | collective-permute-start | bytes 1928 | tf_op jit(solution)/shard_map/ppermute | solution.py:31
  100.6 2.4 %collective-permute-start.19 = (bf16[160,1792]{1,0:T(8,128)(2,1)S(1)}, bf16[160,1792]{1,0:T(8,128)(2,1)S(1)}, u32[]{:S(2)}, u32[]{:S(2)}) collective-permute-start(bf16[160,1792]{1,0:T(8,128)(2,1)S(1)} %fusion.22), channel_id=1, source_target_pairs={{0,1},{1,0},{2,3},{3,2},{4,5},{5,4},{6,7},{7,6},{8,9},{9,8},{10,11... | collective-permute-start | bytes 1720328 | tf_op jit(solution)/shard_map/ppermute | solution.py:31
  104.6 16.2 %collective-permute-start.21 = (bf16[160,1920]{1,0:T(8,128)(2,1)S(1)}, bf16[160,1920]{1,0:T(8,128)(2,1)S(1)}, u32[]{:S(2)}, u32[]{:S(2)}) collective-permute-start(bf16[160,1920]{1,0:T(8,128)(2,1)S(1)} %pad_maximum_fusion.5), channel_id=1, source_target_pairs={{0,2},{1,3},{2,4},{3,5},{4,6},{5,7},{6,0},{7,1},{8,10},{9,11},{10,... | collective-permute-start | bytes 1843208 | tf_op jit(solution)/shard_map/ppermute | solution.py:27
  104.8 15.9 %collective-permute-start.22 = (bf16[160,1920]{1,0:T(8,128)(2,1)S(1)}, bf16[160,1920]{1,0:T(8,128)(2,1)S(1)}, u32[]{:S(2)}, u32[]{:S(2)}) collective-permute-start(bf16[160,1920]{1,0:T(8,128)(2,1)S(1)} %pad_maximum_fusion.6), channel_id=1, source_target_pairs={{0,6},{1,7},{2,0},{3,1},{4,2},{5,3},{6,4},{7,5},{8,14},{9,15},{10,... | collective-permute-start | bytes 1843208 | tf_op jit(solution)/shard_map/ppermute | solution.py:27
  120.9 9.1 %collective-permute-start.23 = (bf16[80,1920]{1,0:T(8,128)(2,1)S(1)}, bf16[80,1920]{1,0:T(8,128)(2,1)S(1)}, u32[]{:S(2)}, u32[]{:S(2)}) collective-permute-start(bf16[80,1920]{1,0:T(8,128)(2,1)S(1)} %get-tuple-element.58), channel_id=1, source_target_pairs={{0,6},{1,7},{2,0},{3,1},{4,2},{5,3},{6,4},{7,5},{8,14},{9,15},{10,... | collective-permute-start | bytes 921608 | tf_op jit(solution)/shard_map/ppermute | solution.py:27
  123.4 8.1 %collective-permute-start.25 = (bf16[80,1920]{1,0:T(8,128)(2,1)S(1)}, bf16[80,1920]{1,0:T(8,128)(2,1)S(1)}, u32[]{:S(2)}, u32[]{:S(2)}) collective-permute-start(bf16[80,1920]{1,0:T(8,128)(2,1)S(1)} %get-tuple-element.59), channel_id=1, source_target_pairs={{0,2},{1,3},{2,4},{3,5},{4,6},{5,7},{6,0},{7,1},{8,10},{9,11},{10,... | collective-permute-start | bytes 921608 | tf_op jit(solution)/shard_map/ppermute | solution.py:27
  131.8 8.6 %collective-permute-start.24 = (bf16[40,1920]{1,0:T(8,128)(2,1)S(1)}, bf16[40,1920]{1,0:T(8,128)(2,1)S(1)}, u32[]{:S(2)}, u32[]{:S(2)}) collective-permute-start(bf16[40,1920]{1,0:T(8,128)(2,1)S(1)} %get-tuple-element.97), channel_id=1, source_target_pairs={{0,24},{8,0},{16,8},{24,16},{32,56},{40,32},{48,40},{56,48},{64,88... | collective-permute-start | bytes 460808 | tf_op jit(solution)/shard_map/ppermute | solution.py:22
  131.9 8.5 %collective-permute-start.26 = (bf16[40,1920]{1,0:T(8,128)(2,1)S(1)}, bf16[40,1920]{1,0:T(8,128)(2,1)S(1)}, u32[]{:S(2)}, u32[]{:S(2)}) collective-permute-start(bf16[40,1920]{1,0:T(8,128)(2,1)S(1)} %get-tuple-element.98), channel_id=1, source_target_pairs={{0,16},{8,24},{16,0},{24,8},{32,48},{40,56},{48,32},{56,40},{64,80... | collective-permute-start | bytes 460808 | tf_op jit(solution)/shard_map/ppermute | solution.py:22
  132.6 7.8 %collective-permute-start.27 = (bf16[40,1920]{1,0:T(8,128)(2,1)S(1)}, bf16[40,1920]{1,0:T(8,128)(2,1)S(1)}, u32[]{:S(2)}, u32[]{:S(2)}) collective-permute-start(bf16[40,1920]{1,0:T(8,128)(2,1)S(1)} %get-tuple-element.99), channel_id=1, source_target_pairs={{0,8},{8,16},{16,24},{24,0},{32,40},{40,48},{48,56},{56,32},{64,72... | collective-permute-start | bytes 460808 | tf_op jit(solution)/shard_map/ppermute | solution.py:22
  140.8 9.6 %collective-permute-start.28 = (bf16[32,1920]{1,0:T(8,128)(2,1)S(1)}, bf16[32,1920]{1,0:T(8,128)(2,1)S(1)}, u32[]{:S(2)}, u32[]{:S(2)}) collective-permute-start(bf16[32,1920]{1,0:T(8,128)(2,1)S(1)} %get-tuple-element.90), channel_id=1, source_target_pairs={{0,96},{8,104},{16,112},{24,120},{32,0},{40,8},{48,16},{56,24},{64... | collective-permute-start | bytes 368648 | tf_op jit(solution)/shard_map/ppermute | solution.py:17
  143.8 6.6 %collective-permute-start.30 = (bf16[32,1920]{1,0:T(8,128)(2,1)S(1)}, bf16[32,1920]{1,0:T(8,128)(2,1)S(1)}, u32[]{:S(2)}, u32[]{:S(2)}) collective-permute-start(bf16[32,1920]{1,0:T(8,128)(2,1)S(1)} %get-tuple-element.91), channel_id=1, source_target_pairs={{0,64},{8,72},{16,80},{24,88},{32,96},{40,104},{48,112},{56,120},{... | collective-permute-start | bytes 368648 | tf_op jit(solution)/shard_map/ppermute | solution.py:17
  144.0 6.4 %collective-permute-start.29 = (bf16[32,1920]{1,0:T(8,128)(2,1)S(1)}, bf16[32,1920]{1,0:T(8,128)(2,1)S(1)}, u32[]{:S(2)}, u32[]{:S(2)}) collective-permute-start(bf16[32,1920]{1,0:T(8,128)(2,1)S(1)} %get-tuple-element.92), channel_id=1, source_target_pairs={{0,32},{8,40},{16,48},{24,56},{32,64},{40,72},{48,80},{56,88},{64,... | collective-permute-start | bytes 368648 | tf_op jit(solution)/shard_map/ppermute | solution.py:17
  150.5 5.7 %collective-permute-start.31 = (bf16[16,1792]{1,0:T(8,128)(2,1)S(1)}, bf16[16,1792]{1,0:T(8,128)(2,1)S(1)}, u32[]{:S(2)}, u32[]{:S(2)}) collective-permute-start(bf16[16,1792]{1,0:T(8,128)(2,1)S(1)} %slice.192), channel_id=1, source_target_pairs={{0,1},{1,0},{2,3},{3,2},{4,5},{5,4},{6,7},{7,6},{8,9},{9,8},{10,11... | collective-permute-start | bytes 172040 | tf_op jit(solution)/shard_map/ppermute | solution.py:31
